TPU v7x, 512 devices: a whole 4x8x8 slice. The times are simulated.
512 devices in a mesh: rep: 32 (over y_hi, x, core), grp: 16 (over z, y_lo).
Axes of the slice: x: 4, y: 8 (y_hi: 4, y_lo: 2; y = y_hi * 2 + y_lo), z: 8, core: 2. Of those that a mesh axis runs over, the one named last changes fastest.
Arguments:
- q_nope: bfloat16 [1024, 2, 128, 128], P('rep', None, 'grp'), may hold values from -6 to 6
- q_rope: bfloat16 [1024, 2, 128, 64], P('rep', None, 'grp'), may hold values from -48 to 48
- new_latent: bfloat16 [1024, 2, 576], P('rep'), may hold values from -6 to 6
- w_uk: bfloat16 [128, 128, 512], P('grp'), may hold values from -0.5 to 0.5
- w_uv: bfloat16 [128, 512, 128], P('grp'), may hold values from -3 to 3
- prefix_store: bfloat16 [32, 2048, 576], P('rep', 'grp'), may hold values from -6 to 6
- store_order: int32 [32], replicated, may hold values from 0 to 31, each once
- prefix_of_group: int32 [32], replicated, may hold values from 0 to 3
- private_store: bfloat16 [32, 32, 2, 256, 576], P('rep', None, None, 'grp'), may hold values from -6 to 6
- request_source: int32 [1024, 1], P('rep'), may hold values from 0 to 31; in each aligned block of 32 rows (0 to 31, 32 to 63, ...) at most 2 rows name the same one
- private_len: int32 [32, 32], P('rep'), may hold values from 1 to 256, 6144 in all within a row
Outputs:
- head_values: bfloat16 [1024, 2, 128, 128], P('rep', None, 'grp')
Inputs may be any that keep to these rules, and one draw needn't show every extreme that they name: `request_source`: within the 32 rows of one decode group no source is named more than 2 times.
All inputs are finite; a program needn't handle non-finite values.
Results may differ from a plain program's by a relative error of at most 0.02.
Values may be sent and summed in bfloat16 or wider, within the bound.
A program may use at most 64 MiB of HBM per device.

v0:
```python
import jax
import jax.numpy as jnp
from jax import lax
from jax.sharding import PartitionSpec as P

NPREF = 4


score_scale = 192.0 ** (-0.5)
very_negative = -1e30


def spread(value, axis, source):
    kept = jnp.where(lax.axis_index(axis) == source, value, 0).astype(value.dtype)
    return lax.psum(kept, axis)


def absorb(state, scores, usable, value_fn):
    running_max, running_sum, weighted = state
    scores = jnp.where(usable, scores, very_negative)
    new_max = jnp.maximum(running_max, jnp.max(scores, axis=-1))
    weights = jnp.where(usable, jnp.exp(scores - new_max[..., None]), 0.0)
    rescale = jnp.exp(running_max - new_max)
    new_sum = running_sum * rescale + jnp.sum(weights, axis=-1)
    new_weighted = weighted * rescale[..., None] + value_fn(weights.astype(jnp.bfloat16))
    return (new_max, new_sum, new_weighted)


def per_request(state, q_lat, q_rope, key_rows, usable, latent_width):
    scores = jnp.einsum(
        "rthc,rkc->rthk", q_lat, key_rows[..., :latent_width], preferred_element_type=jnp.float32
    )
    scores = (
        scores
        + jnp.einsum(
            "rthc,rkc->rthk",
            q_rope,
            key_rows[..., latent_width:],
            preferred_element_type=jnp.float32,
        )
    ) * score_scale

    def value_fn(weights):
        return jnp.einsum(
            "rthk,rkc->rthc",
            weights,
            key_rows[..., :latent_width],
            preferred_element_type=jnp.float32,
        )

    return absorb(state, scores, usable, value_fn)


def empty_state(requests, steps, heads, latent_width):
    return (
        jnp.full((requests, steps, heads), very_negative, jnp.float32),
        jnp.zeros((requests, steps, heads), jnp.float32),
        jnp.zeros((requests, steps, heads, latent_width), jnp.float32),
    )


def shards(
    q_nope,
    q_rope,
    new_latent,
    w_uk,
    w_uv,
    prefix_store,
    store_order,
    prefix_of_group,
    private_store,
    request_source,
    private_len,
):
    latent_width = w_uk.shape[2]
    requests, steps, heads = (q_nope.shape[0], q_nope.shape[1], q_nope.shape[2])
    q_lat = jnp.einsum("rthn,hnc->rthc", q_nope, w_uk, preferred_element_type=jnp.float32).astype(
        jnp.bfloat16
    )
    group_id = lax.axis_index("rep")
    wanted = prefix_of_group[group_id]
    shared = jnp.zeros_like(prefix_store[0])
    for prefix_id in range(NPREF):
        arrived = spread(prefix_store[0], "rep", store_order[prefix_id])
        shared = jnp.where(wanted == prefix_id, arrived, shared)
    state = empty_state(requests, steps, heads, latent_width)
    shard_rows = lax.all_gather(shared, "grp", axis=0, tiled=True)
    for key_start in range(0, shard_rows.shape[0], 512):
        key_block = shard_rows[key_start : key_start + 512]
        scores = jnp.einsum(
            "rthc,kc->rthk", q_lat, key_block[:, :latent_width], preferred_element_type=jnp.float32
        )
        scores = (
            scores
            + jnp.einsum(
                "rthc,kc->rthk",
                q_rope,
                key_block[:, latent_width:],
                preferred_element_type=jnp.float32,
            )
        ) * score_scale

        def value_fn(weights, key_block=key_block):
            return jnp.einsum(
                "rthk,kc->rthc",
                weights,
                key_block[:, :latent_width],
                preferred_element_type=jnp.float32,
            )

        state = absorb(state, scores, True, value_fn)
    received = lax.all_to_all(private_store, "rep", split_axis=1, concat_axis=0, tiled=True)
    capacity = private_store.shape[2]
    received = received.reshape(-1, received.shape[3], received.shape[4])
    source_ids = request_source[:, 0]
    order_ids = jnp.arange(requests, dtype=jnp.int32)
    earlier = (source_ids[:, None] == source_ids[None, :]) & (
        order_ids[None, :] < order_ids[:, None]
    )
    slot_index = source_ids * capacity + jnp.sum(earlier, axis=1)
    live_rows = received[slot_index]
    lengths = private_len[0]
    shard_rows = lax.all_gather(live_rows, "grp", axis=1, tiled=True)
    positions = jnp.arange(shard_rows.shape[1], dtype=jnp.int32)
    usable = (positions[None, :] < lengths[:, None])[:, None, None, :]
    state = per_request(state, q_lat, q_rope, shard_rows, usable, latent_width)
    causal = (jnp.arange(steps)[:, None] >= jnp.arange(steps)[None, :])[None, :, None, :]
    state = per_request(state, q_lat, q_rope, new_latent, causal, latent_width)
    attended = (state[2] / state[1][..., None]).astype(jnp.bfloat16)
    return jnp.einsum("rthc,hcv->rthv", attended, w_uv, preferred_element_type=jnp.float32).astype(
        jnp.bfloat16
    )


def solution(mesh):
    in_specs = (
        P("rep", None, "grp", None),
        P("rep", None, "grp", None),
        P("rep", None, None),
        P("grp", None, None),
        P("grp", None, None),
        P("rep", "grp", None),
        P(),
        P(),
        P("rep", None, None, "grp", None),
        P("rep", None),
        P("rep", None),
    )
    out_specs = P("rep", None, "grp", None)
    return jax.shard_map(shards, mesh=mesh, in_specs=in_specs, out_specs=out_specs, check_vma=False)
```

profile of v0, /device:TPU:6, one launch (start us, length us, event | category | flops | bytes accessed | tf_op | source)
XLA Modules:
  0.0 672.3 jit_solution(17605148280163711545)
XLA Ops:
  6.5 1.1 copy.146
  7.7 1.5 fusion.102
  11.7 0.9 select_bitcast_fusion
  12.7 1.2 dynamic_slice.3
  16.5 276.1 %all-reduce.3.cloned.1.call-done = (bf16[128,576]{1,0:T(8,128)(2,1)}, bf16[128,576]{1,0:T(8,128)(2,1)}, bf16[128,576]{1,0:T(8,128)(2,1)}, bf16[128,576]{1,0:T(8,128)(2,1)}) async-done(((bf16[128,576]{1,0:T(8,128)(2,1)}, bf16[128,576]{1,0:T(8,128)(2,1)}, bf16[128,576]{1,0:T(8,128)(2,1)}, bf16[128,576]{1,0:T(8,128)(2,1)}), (bf16[128,576]{1,0:T(8,128)(2,1)}, bf16[128,576]{1,0:T(8,128)(2,1)}, ...) | async-done | bytes 589840 | tf_op jit(solution)/shard_map/psum | solution.py:15
  292.6 1.7 select_select_fusion
  294.3 17.0 %all-to-all-start = ((bf16[1,32,2,16,576]{4,3,2,0,1:T(8,128)(2,1)}), bf16[1,32,2,16,576]{4,3,2,0,1:T(8,128)(2,1)S(1)}, u32[]{:S(2)}, u32[]{:S(2)}) async-start(bf16[1,32,2,16,576]{4,3,2,0,1:T(8,128)(2,1)} %bitcast.163), calls=%async_computation | async-start | bytes 2621440 | tf_op jit(solution)/shard_map/all_to_all | solution.py:112
  311.6 44.4 %all-to-all-done = bf16[1,32,2,16,576]{4,3,2,0,1:T(8,128)(2,1)S(1)} async-done(((bf16[1,32,2,16,576]{4,3,2,0,1:T(8,128)(2,1)}), bf16[1,32,2,16,576]{4,3,2,0,1:T(8,128)(2,1)S(1)}, u32[]{:S(2)}, u32[]{:S(2)}) %all-to-all-start) | async-done | bytes 1179680 | tf_op jit(solution)/shard_map/all_to_all | solution.py:112
  356.0 1.5 gather_fusion
  357.9 1.3 fusion.78
  359.2 0.7 fusion.103
  360.0 44.7 %all-gather.4.cloned.1.call-done = bf16[2048,576]{1,0:T(8,128)(2,1)} async-done(((bf16[128,576]{1,0:T(8,128)(2,1)}), bf16[2048,576]{1,0:T(8,128)(2,1)}) %all-gather.4.cloned.1.call-update) | async-done | bytes 2359312 | tf_op jit(solution)/shard_map/all_gather | solution.py:87
  404.7 1.5 fusion.42
  406.3 2.2 fusion.105
  408.6 1.5 fusion.44
  410.1 2.2 fusion.106
  412.4 1.5 fusion.46
  413.9 2.2 fusion.107
  416.2 1.5 fusion.48
  417.7 1.3 fusion.108
  419.1 215.2 %all-gather.6.cloned.1.call-done = bf16[32,256,576]{2,1,0:T(8,128)(2,1)} async-done(((bf16[32,16,576]{2,1,0:T(8,128)(2,1)}), bf16[32,256,576]{2,1,0:T(8,128)(2,1)}) %all-gather.6.cloned.1.call-update) | async-done | bytes 9437200 | tf_op jit(solution)/shard_map/all_gather | solution.py:123
  634.3 5.6 fusion.1
  639.9 3.1 fusion.104
  643.4 1.4 fusion.86
  645.1 1.3 fusion.72
  646.6 2.3 fusion.41
  649.0 2.3 fusion.39
  651.4 1.0 fusion.37
  653.1 5.9 fusion
  659.5 0.5 copy-done.5
  661.3 3.7 fusion.27
  665.0 0.7 copy.193
  (65 shorter events, 4.5 us)
Async XLA Ops:
  6.5 351.0 %copy-start = (bf16[8,128,512]{2,1,0:T(8,128)(2,1)S(1)}, bf16[8,128,512]{2,1,0:T(8,128)(2,1)}, u32[]{:S(2)}) copy-start(bf16[8,128,512]{2,1,0:T(8,128)(2,1)} %param.14) | copy-start | bytes 3145732
  6.5 286.1 %all-reduce.3.cloned.1.call-start = ((), (), s32[]{:S(2)}) async-start(), calls=%async_computation.3 | async-start | bytes 1310720 | tf_op jit(solution)/shard_map/psum | solution.py:15
  7.7 303.7 %copy-start.10 = (s32[32,1]{0,1:T(1,128)S(1)}, s32[32,1]{0,1:T(1,128)}, u32[]{:S(2)}) copy-start(s32[32,1]{0,1:T(1,128)} %param.20) | copy-start | bytes 388
  12.6 392.1 %all-gather.4.cloned.1.call-start = ((), (), s32[]{:S(2)}) async-start(), calls=%async_computation.1 | async-start | bytes 2785280 | tf_op jit(solution)/shard_map/all_gather | solution.py:87
  292.6 64.9 %copy-start.7 = (bf16[32,2,8,128]{3,2,1,0:T(8,128)(2,1)S(1)}, bf16[32,2,8,128]{3,2,1,0:T(8,128)(2,1)}, u32[]{:S(2)}) copy-start(bf16[32,2,8,128]{3,2,1,0:T(8,128)(2,1)} %param.11) | copy-start | bytes 393220
  294.3 63.6 %copy-start.8 = (bf16[32,2,576]{2,1,0:T(2,128)(2,1)S(1)}, bf16[32,2,576]{2,1,0:T(2,128)(2,1)}, u32[]{:S(2)}) copy-start(bf16[32,2,576]{2,1,0:T(2,128)(2,1)} %param.13) | copy-start | bytes 221188
  294.3 61.7 %all-to-all-start = ((bf16[1,32,2,16,576]{4,3,2,0,1:T(8,128)(2,1)}), bf16[1,32,2,16,576]{4,3,2,0,1:T(8,128)(2,1)S(1)}, u32[]{:S(2)}, u32[]{:S(2)}) async-start(bf16[1,32,2,16,576]{4,3,2,0,1:T(8,128)(2,1)} %bitcast.163), calls=%async_computation | async-start | bytes 2621440 | tf_op jit(solution)/shard_map/all_to_all | solution.py:112
  311.3 47.8 %copy-start.2 = (bf16[32,2,8,64]{3,2,1,0:T(8,128)(2,1)S(1)}, bf16[32,2,8,64]{3,2,1,0:T(8,128)(2,1)}, u32[]{:S(2)}) copy-start(bf16[32,2,8,64]{3,2,1,0:T(8,128)(2,1)} %param.12) | copy-start | bytes 196612
  311.4 322.9 %all-gather.6.cloned.1.call-start = ((), (), s32[]{:S(2)}) async-start(), calls=%async_computation.2 | async-start | bytes 11141120 | tf_op jit(solution)/shard_map/all_gather | solution.py:123
  356.0 4.0 copy-start.9
  643.4 8.0 %copy-start.1 = (f32[32,2,8,512]{3,2,1,0:T(8,128)S(1)}, f32[32,2,8,512]{3,2,1,0:T(8,128)}, u32[]{:S(2)}) copy-start(f32[32,2,8,512]{3,2,1,0:T(8,128)} %get-tuple-element.47) | copy-start | bytes 3145732
  653.1 5.9 copy-start.3
  659.0 1.0 copy-start.5
  659.0 1.5 copy-start.4
  660.1 1.3 copy-start.6
Sparse Core Ops, SparseCore 0:
  12.7 279.8 all-reduce.2
  294.9 109.7 all-gather.3
  407.0 227.1 all-gather.5
where the time goes:
time: 674 us; the launch traced here: 672 us
  waiting for transfers between devices  580 us (86%)
  matrix products  37.6 us (6%)
  between operations  18.5 us (3%)
  starting transfers between devices  17.1 us (3%)
  other arithmetic  10.3 us (2%)
  local copies, waits for them, and re-layouts  8.36 us (1%)
    psum x1, waiting for transfers between devices, spread(): return lax.psum(kept, axis)  276 us
    all_gather x1, waiting for transfers between devices, shards(): shard_rows = lax.all_gather(live_rows, 'grp', axis=1, tiled=True)  215 us
    all_gather x1, waiting for transfers between devices, shards(): shard_rows = lax.all_gather(shared, 'grp', axis=0, tiled=True)  44.7 us
    all_to_all x1, waiting for transfers between devices, shards(): lax.all_to_all(private_store, 'rep', split_axis=1, concat_axis=0, tiled=T...  44.4 us
    all_to_all x1, starting transfers between devices, shards(): lax.all_to_all(private_store, 'rep', split_axis=1, concat_axis=0, tiled=T...  17 us
  transfers between devices with their start and end apart: 4, of which 4 were waited for; matrix products, arithmetic and copies ran while one was open for 3% of the time, Pallas kernels for 0%

commit v1 on v0

v1 whole, which is shorter than its diff:
```python
import jax
import jax.numpy as jnp
from jax import lax
from jax.sharding import PartitionSpec as P

NPREF = 4

score_scale = 192.0 ** (-0.5)
very_negative = -1e30


def spread_prefix(prefix_shard, store_order, prefix_of_group, groups):
    rows, width = prefix_shard.shape
    pieces = prefix_shard.reshape(groups, rows // groups * width)
    arrived = lax.all_to_all(pieces, "rep", split_axis=0, concat_axis=0, tiled=True)
    chosen = arrived[store_order[prefix_of_group]]
    mine = lax.all_to_all(chosen, "rep", split_axis=0, concat_axis=0, tiled=True)
    return mine.reshape(rows, width)


def in_three(value):
    high = lax.reduce_precision(value, 8, 7)
    middle = lax.reduce_precision(value - high, 8, 7)
    low = value - high - middle
    return [part.astype(jnp.bfloat16) for part in (high, middle, low)]


def private_part(q, keys, new_keys, lengths, latent_width):
    owned, steps, heads, _ = q.shape
    scores = jnp.einsum("rthc,rkc->rthk", q, keys, preferred_element_type=jnp.float32) * score_scale
    positions = jnp.arange(keys.shape[1], dtype=jnp.int32)
    usable = (positions[None, :] < lengths[:, None])[:, None, None, :]
    scores = jnp.where(usable, scores, very_negative)
    new_scores = jnp.einsum("rthc,rkc->rthk", q, new_keys, preferred_element_type=jnp.float32) * score_scale
    causal = (jnp.arange(steps)[:, None] >= jnp.arange(steps)[None, :])[None, :, None, :]
    new_scores = jnp.where(causal, new_scores, very_negative)
    top = jnp.maximum(jnp.max(scores, axis=-1), jnp.max(new_scores, axis=-1))
    e = jnp.where(usable, jnp.exp(scores - top[..., None]), 0.0)
    new_e = jnp.where(causal, jnp.exp(new_scores - top[..., None]), 0.0)
    total = jnp.sum(e, axis=-1) + jnp.sum(new_e, axis=-1)
    weighted = jnp.einsum(
        "rthk,rkc->rthc", e.astype(jnp.bfloat16), keys[..., :latent_width], preferred_element_type=jnp.float32
    ) + jnp.einsum(
        "rthk,rkc->rthc", new_e.astype(jnp.bfloat16), new_keys[..., :latent_width], preferred_element_type=jnp.float32
    )
    return weighted / total[..., None], top + jnp.log(total)


def shards(
    q_nope,
    q_rope,
    new_latent,
    w_uk,
    w_uv,
    prefix_store,
    store_order,
    prefix_of_group,
    private_store,
    request_source,
    private_len,
):
    latent_width = w_uk.shape[2]
    requests, steps, heads = (q_nope.shape[0], q_nope.shape[1], q_nope.shape[2])
    groups, capacity = private_store.shape[1], private_store.shape[2]
    q_lat = jnp.einsum("rthn,hnc->rthc", q_nope, w_uk, preferred_element_type=jnp.float32).astype(
        jnp.bfloat16
    )
    q = jnp.concatenate([q_lat, q_rope], axis=-1)

    received = lax.all_to_all(private_store, "rep", split_axis=1, concat_axis=0, tiled=True)
    received = received.reshape(-1, received.shape[3], received.shape[4])
    source_ids = request_source[:, 0]
    order_ids = jnp.arange(requests, dtype=jnp.int32)
    earlier = (source_ids[:, None] == source_ids[None, :]) & (
        order_ids[None, :] < order_ids[:, None]
    )
    slot_index = source_ids * capacity + jnp.sum(earlier, axis=1)
    pages = lax.all_to_all(received[slot_index], "grp", split_axis=0, concat_axis=1, tiled=True)
    owned = pages.shape[0]

    q_owned = lax.all_to_all(q, "grp", split_axis=0, concat_axis=2, tiled=True)
    first = lax.axis_index("grp") * owned
    new_keys = lax.dynamic_slice_in_dim(new_latent, first, owned, 0)
    lengths = lax.dynamic_slice_in_dim(private_len[0], first, owned, 0)
    part, part_lse = private_part(q_owned, pages, new_keys, lengths, latent_width)
    back = jnp.concatenate([part.astype(jnp.bfloat16)] + [x[..., None] for x in in_three(part_lse)], axis=-1)
    back = lax.all_to_all(back, "grp", split_axis=2, concat_axis=0, tiled=True)
    part = back[..., :latent_width].astype(jnp.float32)
    part_lse = jnp.sum(back[..., latent_width:].astype(jnp.float32), axis=-1)

    shard = spread_prefix(prefix_store[0], store_order, prefix_of_group, groups)
    shared = lax.all_gather(shard, "grp", axis=0, tiled=True)
    scores = jnp.einsum("rthc,kc->rthk", q, shared, preferred_element_type=jnp.float32) * score_scale
    top = jnp.max(scores, axis=-1)
    e = jnp.exp(scores - top[..., None])
    total = jnp.sum(e, axis=-1)
    weighted = jnp.einsum(
        "rthk,kc->rthc", e.astype(jnp.bfloat16), shared[:, :latent_width], preferred_element_type=jnp.float32
    )
    both = jnp.maximum(top, part_lse)
    scale, part_scale = jnp.exp(top - both), jnp.exp(part_lse - both)
    attended = (weighted * scale[..., None] + part * part_scale[..., None]) / (total * scale + part_scale)[..., None]
    return jnp.einsum(
        "rthc,hcv->rthv", attended.astype(jnp.bfloat16), w_uv, preferred_element_type=jnp.float32
    ).astype(jnp.bfloat16)


def solution(mesh):
    in_specs = (
        P("rep", None, "grp", None),
        P("rep", None, "grp", None),
        P("rep", None, None),
        P("grp", None, None),
        P("grp", None, None),
        P("rep", "grp", None),
        P(),
        P(),
        P("rep", None, None, "grp", None),
        P("rep", None),
        P("rep", None),
    )
    out_specs = P("rep", None, "grp", None)
    return jax.shard_map(shards, mesh=mesh, in_specs=in_specs, out_specs=out_specs, check_vma=False)
```

time: 674 us -> 216 us (0.32)
  waiting for transfers between devices: 580 us -> 89.6 us
  blocking collectives: 0 us -> 45.7 us
  matrix products: 37.6 us -> 14.7 us
  starting transfers between devices: 17.1 us -> 30.6 us
    psum x1 -> x0, waiting for transfers between devices: 276 us -> none  [spread(): return lax.psum(kept, axis)]
    all_gather x2 -> x1, waiting for transfers between devices: 260 us -> 13.6 us  [shards(): shared = lax.all_gather(shard, 'grp', axis=0, tiled=True)]
    all_to_all x0 -> x2, blocking collectives: none -> 45.7 us  [the longest x1 31 us: shards(): back = lax.all_to_all(back, 'grp', split_axis=2, concat_axis=0, tiled=True)]
    all_to_all x0 -> x3, waiting for transfers between devices: none -> 43.6 us  [the longest x1 21 us: shards(): lax.all_to_all(received[slot_index], 'grp', split_axis=0, concat_axis=1,...]
    all_to_all x0 -> x3, starting transfers between devices: none -> 24.8 us  [the longest x1 11.1 us: shards(): q_owned = lax.all_to_all(q, 'grp', split_axis=0, concat_axis=2, tiled=True)]
    dot_general x18 -> x6, matrix products: 37.3 us -> 14.4 us  [the longest x1 5.47 us: shards(): jnp.einsum('rthc,kc->rthk', q, shared, preferred_element_type=jnp.float32)]
    all_to_all x1, waiting for transfers between devices: 44.4 us -> 32.4 us  [shards(): lax.all_to_all(private_store, 'rep', split_axis=1, concat_axis=0, tiled=T...]
    all_to_all x1, starting transfers between devices: 17 us -> 5.68 us  [shards(): lax.all_to_all(private_store, 'rep', split_axis=1, concat_axis=0, tiled=T...]
  transfers between devices with their start and end apart: 4 -> 5, of which waited for: 4 -> 5; matrix products, arithmetic and copies ran while one was open for 3% -> 6% of each run, Pallas kernels for 0% -> 0%
where the time goes in v1:
time: 216 us; the launch traced here: 215 us
  waiting for transfers between devices  89.6 us (41%)
  blocking collectives  45.7 us (21%)
  starting transfers between devices  30.6 us (14%)
  matrix products  14.7 us (7%)
  between operations  13.7 us (6%)
  local copies, waits for them, and re-layouts  11.5 us (5%)
  other arithmetic  9.19 us (4%)
    all_to_all x1, waiting for transfers between devices, shards(): lax.all_to_all(private_store, 'rep', split_axis=1, concat_axis=0, tiled=T...  32.4 us
    all_to_all x1, blocking collectives, shards(): back = lax.all_to_all(back, 'grp', split_axis=2, concat_axis=0, tiled=True)  31 us
    all_to_all x1, waiting for transfers between devices, shards(): lax.all_to_all(received[slot_index], 'grp', split_axis=0, concat_axis=1,...  21 us
    all_to_all x1, waiting for transfers between devices, shards(): q_owned = lax.all_to_all(q, 'grp', split_axis=0, concat_axis=2, tiled=True)  14.9 us
    all_to_all x1, blocking collectives, spread_prefix(): lax.all_to_all(chosen, 'rep', split_axis=0, concat_axis=0, tiled=True)  14.7 us
    all_gather x1, waiting for transfers between devices, shards(): shared = lax.all_gather(shard, 'grp', axis=0, tiled=True)  13.6 us
    all_to_all x1, starting transfers between devices, shards(): q_owned = lax.all_to_all(q, 'grp', split_axis=0, concat_axis=2, tiled=True)  11.1 us
    all_to_all x1, starting transfers between devices, spread_prefix(): lax.all_to_all(pieces, 'rep', split_axis=0, concat_axis=0, tiled=True)  10.2 us
  transfers between devices with their start and end apart: 5, of which 5 were waited for; matrix products, arithmetic and copies ran while one was open for 6% of the time, Pallas kernels for 0%

profile of v1, /device:TPU:6, one launch (start us, length us, event | category | flops | bytes accessed | tf_op | source)
XLA Modules:
  0.0 215.0 jit_solution(1890036370888471903)
XLA Ops:
  6.5 1.2 copy.138
  8.4 1.5 reduce.1
  10.0 0.7 reshape.216
  10.7 10.2 %all-to-all-start = ((bf16[32,2,1152]{2,1,0:T(2,128)(2,1)}), bf16[32,2,1152]{2,1,0:T(2,128)(2,1)S(1)}, u32[]{:S(2)}, u32[]{:S(2)}) async-start(bf16[32,2,1152]{2,1,0:T(2,128)(2,1)} %reshape.216), calls=%async_computation | async-start | bytes 294912 | tf_op jit(solution)/shard_map/all_to_all | solution.py:15
  20.9 0.7 compare_select_fusion.2
  21.6 0.7 gather_fusion
  22.3 7.7 %all-to-all-done = bf16[32,2,1152]{2,1,0:T(2,128)(2,1)S(1)} async-done(((bf16[32,2,1152]{2,1,0:T(2,128)(2,1)}), bf16[32,2,1152]{2,1,0:T(2,128)(2,1)S(1)}, u32[]{:S(2)}, u32[]{:S(2)}) %all-to-all-start) | async-done | bytes 147488 | tf_op jit(solution)/shard_map/all_to_all | solution.py:15
  30.2 0.7 gather_fusion.1
  30.8 0.7 reduce.2
  31.6 14.7 %all_to_all.85 = bf16[32,2,1152]{2,1,0:T(2,128)(2,1)S(1)} all-to-all(bf16[32,2,1152]{2,1,0:T(2,128)(2,1)S(1)} %reshape.218), channel_id=1, replica_groups=mesh['rep'=32,'grp'=16] {'rep'}, dimensions={0} | all-to-all | bytes 294912 | tf_op jit(solution)/shard_map/all_to_all | solution.py:17
  46.3 5.7 %all-to-all-start.3 = ((bf16[1,32,2,16,576]{4,3,2,0,1:T(8,128)(2,1)}), bf16[1,32,2,16,576]{4,3,2,0,1:T(8,128)(2,1)S(1)}, u32[]{:S(2)}, u32[]{:S(2)}) async-start(bf16[1,32,2,16,576]{4,3,2,0,1:T(8,128)(2,1)} %bitcast.114), calls=%async_computation.3 | async-start | bytes 2621440 | tf_op jit(solution)/shard_map/all_to_all | solution.py:70
  52.4 1.4 copy.145
  53.8 32.4 %all-to-all-done.3 = bf16[1,32,2,16,576]{4,3,2,0,1:T(8,128)(2,1)S(1)} async-done(((bf16[1,32,2,16,576]{4,3,2,0,1:T(8,128)(2,1)}), bf16[1,32,2,16,576]{4,3,2,0,1:T(8,128)(2,1)S(1)}, u32[]{:S(2)}, u32[]{:S(2)}) %all-to-all-start.3) | async-done | bytes 1179680 | tf_op jit(solution)/shard_map/all_to_all | solution.py:70
  86.2 11.1 %all-to-all-start.2 = ((bf16[32,2,8,576]{3,1,2,0:T(2,128)(2,1)}), bf16[32,2,8,576]{3,1,2,0:T(2,128)(2,1)}, u32[]{:S(2)}, u32[]{:S(2)}) async-start(bf16[32,2,8,576]{3,1,2,0:T(2,128)(2,1)} %copy.145), calls=%async_computation.2 | async-start | bytes 1310720 | tf_op jit(solution)/shard_map/all_to_all | solution.py:81
  97.4 0.9 reduce
  98.5 0.8 copy.141
  99.5 1.5 gather_fusion.2
  101.0 14.9 %all-to-all-done.2 = bf16[32,2,8,576]{3,1,2,0:T(2,128)(2,1)} async-done(((bf16[32,2,8,576]{3,1,2,0:T(2,128)(2,1)}), bf16[32,2,8,576]{3,1,2,0:T(2,128)(2,1)}, u32[]{:S(2)}, u32[]{:S(2)}) %all-to-all-start.2) | async-done | bytes 589856 | tf_op jit(solution)/shard_map/all_to_all | solution.py:81
  115.8 3.6 %all-to-all-start.4 = ((bf16[32,16,576]{2,1,0:T(8,128)(2,1)}), bf16[32,16,576]{2,1,0:T(8,128)(2,1)S(1)}, u32[]{:S(2)}, u32[]{:S(2)}) async-start(bf16[32,16,576]{2,1,0:T(8,128)(2,1)} %gather_fusion.2), calls=%async_computation.4 | async-start | bytes 1310720 | tf_op jit(solution)/shard_map/all_to_all | solution.py:78
  119.6 1.4 fusion.58
  121.0 21.0 %all-to-all-done.4 = bf16[32,16,576]{2,1,0:T(8,128)(2,1)S(1)} async-done(((bf16[32,16,576]{2,1,0:T(8,128)(2,1)}), bf16[32,16,576]{2,1,0:T(8,128)(2,1)S(1)}, u32[]{:S(2)}, u32[]{:S(2)}) %all-to-all-start.4) | async-done | bytes 589856 | tf_op jit(solution)/shard_map/all_to_all | solution.py:78
  142.1 1.6 fusion.57
  145.1 1.1 fusion.13
  146.3 0.7 copy.157
  147.0 31.0 %all_to_all.86 = bf16[2,2,128,515]{3,1,0,2:T(2,128)(2,1)S(1)} all-to-all(bf16[2,2,128,515]{3,1,0,2:T(2,128)(2,1)S(1)} %copy.157), channel_id=1, replica_groups=mesh['rep'=32,'grp'=16] {'grp'}, dimensions={2} | all-to-all | bytes 1054720 | tf_op jit(solution)/shard_map/all_to_all | solution.py:87
  178.0 0.6 copy.217
  178.6 0.5 all_to_all.77
  179.3 13.6 %all-gather.2.cloned.1.call-done = bf16[2048,576]{0,1:T(8,128)(2,1)} async-done(((bf16[128,576]{0,1:T(8,128)(2,1)}), bf16[2048,576]{0,1:T(8,128)(2,1)}) %all-gather.2.cloned.1.call-update) | async-done | bytes 2359312 | tf_op jit(solution)/shard_map/all_gather | solution.py:92
  192.9 5.5 %multiply_reduce_fusion = (f32[32,2,8]{2,1,0:T(2,128)S(1)}, f32[32,2,8,2048]{3,2,1,0:T(8,128)}) fusion(bf16[2048,576]{0,1:T(8,128)(2,1)} %all-gather.2.cloned.1.call-done, bf16[32,2,8,576]{3,0,1,2:T(8,128)(2,1)S(1)} %pad_maximum_fusion), kind=kOutput, calls=%fused_computation.4 | convolution fusion | flops 1210056192 | bytes 7145472 | tf_op jit(solution)/shard_map/rthc,kc->rthk/dot_general | solution.py:93
  198.4 4.4 %fusion = (f32[32,2,8]{2,1,0:T(2,128)S(1)}, bf16[32,2,8,2048]{3,2,1,0:T(8,128)(2,1)}) fusion(f32[32,2,8,2048]{3,2,1,0:T(8,128)} %get-tuple-element.15, f32[32,2,8]{2,1,0:T(2,128)S(1)} %get-tuple-element.14), kind=kLoop, calls=%fused_computation.5 | loop fusion | flops 4193792 | bytes 6295552 | tf_op jit(solution)/shard_map/reduce_sum | solution.py:96
  202.9 4.5 %fusion.16 = bf16[32,2,8,128]{3,0,1,2:T(8,128)(2,1)S(1)} fusion(bf16[8,512,128]{2,1,0:T(8,128)(2,1)} %param.15, bf16[2048,576]{0,1:T(8,128)(2,1)} %all-gather.2.cloned.1.call-done, bf16[32,2,8,2048]{3,2,1,0:T(8,128)(2,1)} %get-tuple-element.11, bf16[32,2,8,515]{3,0,1,2:T(8,128)(2,1)S(1)} %all_to_all.77, f32[32,2,8]{0,1,2:T(2,128)S(1)} %copy.166, ...), kind=kOutput, calls=%fused_computation.22 | convolution fusion | flops 1142489088 | bytes 5922816 | tf_op jit(solution)/shard_map/rthc,hcv->rthv/dot_general | solution.py:103
  207.4 0.7 copy.167
  (51 shorter events, 3.9 us)
Async XLA Ops:
  6.5 45.5 %copy-start = (bf16[8,128,512]{2,1,0:T(8,128)(2,1)S(1)}, bf16[8,128,512]{2,1,0:T(8,128)(2,1)}, u32[]{:S(2)}) copy-start(bf16[8,128,512]{2,1,0:T(8,128)(2,1)} %param.14) | copy-start | bytes 3145732
  6.5 15.0 %copy-start.1 = (s32[32]{0:T(128)S(1)}, s32[32]{0:T(128)}, u32[]{:S(2)}) copy-start(s32[32]{0:T(128)} %param.17) | copy-start | bytes 388
  10.7 19.3 %all-to-all-start = ((bf16[32,2,1152]{2,1,0:T(2,128)(2,1)}), bf16[32,2,1152]{2,1,0:T(2,128)(2,1)S(1)}, u32[]{:S(2)}, u32[]{:S(2)}) async-start(bf16[32,2,1152]{2,1,0:T(2,128)(2,1)} %reshape.216), calls=%async_computation | async-start | bytes 294912 | tf_op jit(solution)/shard_map/all_to_all | solution.py:15
  30.2 21.8 %copy-start.2 = (bf16[32,2,8,64]{3,2,1,0:T(8,128)(2,1)S(1)}, bf16[32,2,8,64]{3,2,1,0:T(8,128)(2,1)}, u32[]{:S(2)}) copy-start(bf16[32,2,8,64]{3,2,1,0:T(8,128)(2,1)} %param.12) | copy-start | bytes 196612
  30.8 21.2 %copy-start.3 = (bf16[32,2,8,128]{3,2,1,0:T(8,128)(2,1)S(1)}, bf16[32,2,8,128]{3,2,1,0:T(8,128)(2,1)}, u32[]{:S(2)}) copy-start(bf16[32,2,8,128]{3,2,1,0:T(8,128)(2,1)} %param.11) | copy-start | bytes 393220
  46.3 39.9 %all-to-all-start.3 = ((bf16[1,32,2,16,576]{4,3,2,0,1:T(8,128)(2,1)}), bf16[1,32,2,16,576]{4,3,2,0,1:T(8,128)(2,1)S(1)}, u32[]{:S(2)}, u32[]{:S(2)}) async-start(bf16[1,32,2,16,576]{4,3,2,0,1:T(8,128)(2,1)} %bitcast.114), calls=%async_computation.3 | async-start | bytes 2621440 | tf_op jit(solution)/shard_map/all_to_all | solution.py:70
  52.4 46.9 %copy-start.4 = (s32[32,1]{0,1:T(1,128)S(1)}, s32[32,1]{0,1:T(1,128)}, u32[]{:S(2)}) copy-start(s32[32,1]{0,1:T(1,128)} %param.20) | copy-start | bytes 388
  86.2 29.7 %all-to-all-start.2 = ((bf16[32,2,8,576]{3,1,2,0:T(2,128)(2,1)}), bf16[32,2,8,576]{3,1,2,0:T(2,128)(2,1)}, u32[]{:S(2)}, u32[]{:S(2)}) async-start(bf16[32,2,8,576]{3,1,2,0:T(2,128)(2,1)} %copy.145), calls=%async_computation.2 | async-start | bytes 1310720 | tf_op jit(solution)/shard_map/all_to_all | solution.py:81
  97.2 22.2 %copy-start.5 = (s32[1,32]{1,0:T(1,128)S(1)}, s32[1,32]{1,0:T(1,128)}, u32[]{:S(2)}) copy-start(s32[1,32]{1,0:T(1,128)} %param.21) | copy-start | bytes 388
  97.2 95.7 %all-gather.2.cloned.1.call-start = ((), (), s32[]{:S(2)}) async-start(), calls=%async_computation.6 | async-start | bytes 2506752 | tf_op jit(solution)/shard_map/all_gather | solution.py:92
  115.8 26.2 %all-to-all-start.4 = ((bf16[32,16,576]{2,1,0:T(8,128)(2,1)}), bf16[32,16,576]{2,1,0:T(8,128)(2,1)S(1)}, u32[]{:S(2)}, u32[]{:S(2)}) async-start(bf16[32,16,576]{2,1,0:T(8,128)(2,1)} %gather_fusion.2), calls=%async_computation.4 | async-start | bytes 1310720 | tf_op jit(solution)/shard_map/all_to_all | solution.py:78
Sparse Core Ops, SparseCore 0:
  100.1 92.7 all-gather.1

commit v2 on v1

v2 whole, which is shorter than its diff:
```python
import functools

import jax
import jax.numpy as jnp
from jax import lax
from jax.experimental import pallas as pl
from jax.experimental.pallas import tpu as pltpu
from jax.sharding import PartitionSpec as P

score_scale = 192.0 ** (-0.5)
very_negative = -1e30
MIB = 1024 * 1024
MESH = pl.DeviceIdType.MESH


def contract_last(a, b):
    return lax.dot_general(a, b, (((1,), (1,)), ((), ())), preferred_element_type=jnp.float32)


def loop(count, body):
    def step(i, carry):
        body(i)
        return carry

    lax.fori_loop(0, count, step, 0)


def remote(src, dst, send, recv, where):
    return pltpu.make_async_remote_copy(
        src_ref=src, dst_ref=dst, send_sem=send, recv_sem=recv, device_id=where, device_id_type=MESH
    )


def greet(groups, members):
    me, mine = lax.axis_index("rep"), lax.axis_index("grp")
    barrier = pltpu.get_barrier_semaphore()

    def along_rep(k):
        pl.semaphore_signal(barrier, inc=1, device_id={"rep": (me + k + 1) % groups}, device_id_type=MESH)

    def along_grp(k):
        pl.semaphore_signal(barrier, inc=1, device_id={"grp": (mine + k + 1) % members}, device_id_type=MESH)

    loop(groups - 1, along_rep)
    loop(members - 1, along_grp)
    pl.semaphore_wait(barrier, groups + members - 2)


class Exchange:
    def __init__(self, axis, peers, out_ref, in_ref, send, recv):
        self.axis, self.peers, self.out_ref, self.in_ref, self.send, self.recv = axis, peers, out_ref, in_ref, send, recv
        self.me = lax.axis_index(axis)

    def peer(self, k):
        return (self.me + k + 1) % self.peers

    def to(self, j):
        return remote(self.out_ref(j), self.in_ref(self.me), self.send(j), self.recv(self.me), {self.axis: j})

    def own(self):
        return pltpu.make_async_copy(self.out_ref(self.me), self.in_ref(self.me), self.recv(self.me))

    def start(self, begin=0, end=None):
        loop((self.peers - 1 if end is None else end) - begin, lambda k: self.to(self.peer(k + begin)).start())

    def arrive(self, j):
        remote(self.out_ref(j), self.in_ref(j), self.send(j), self.recv(j), {self.axis: j}).wait_recv()

    def finish(self):
        self.own().wait()
        loop(self.peers - 1, lambda k: self.arrive(self.peer(k)))

    def drain(self):
        loop(self.peers - 1, lambda k: self.to(self.peer(k)).wait_send())


def prefix_kernel(
    groups,
    members,
    q_lat,
    q_rope,
    store_lat,
    store_rope,
    store_order,
    prefix_of_group,
    out,
    top,
    total,
    one_out,
    one_in,
    two_out,
    two_in,
    pref_lat,
    pref_rope,
    scores,
    one_send,
    one_recv,
    two_send,
    two_recv,
    ring_send,
    ring_recv,
    ring_rope_send,
    ring_rope_recv,
):
    mine = lax.axis_index("grp")
    half = members // 2
    z, y = mine // 2, mine % 2
    latent, rope = q_lat.shape[1], q_rope.shape[1]
    lanes = latent // 4

    def rows_of(j):
        return pl.ds(pl.multiple_of((j // 4) * 16, 16), 16)

    def columns_of(j):
        return pl.ds(pl.multiple_of((j % 4) * lanes, lanes), lanes)

    def cut(j):
        one_out[j, pl.ds(0, 16)] = store_lat[rows_of(j), columns_of(j)]
        one_out[j, pl.ds(16, 16)] = jnp.concatenate([store_rope[rows_of(j)], jnp.zeros((16, lanes - rope), jnp.bfloat16)], axis=1)

    loop(groups, cut)
    greet(groups, members)
    one = Exchange("rep", groups, lambda j: one_out.at[j], lambda j: one_in.at[j], lambda j: one_send.at[j], lambda j: one_recv.at[j])
    two = Exchange("rep", groups, lambda j: two_out.at[j], lambda j: two_in.at[j], lambda j: two_send.at[j], lambda j: two_recv.at[j])
    one.start()
    one.own().start()
    one.finish()

    def choose(j):
        two_out[j] = one_in[store_order[prefix_of_group[j]]]

    loop(groups, choose)
    two.start()
    two.own().start()
    two.finish()

    def place(j):
        pref_lat[mine, rows_of(j), columns_of(j)] = two_in[j, pl.ds(0, 16)]

    def place_rope(b):
        pref_rope[mine, pl.ds(pl.multiple_of(b * 16, 16), 16)] = two_in[4 * b, pl.ds(16, 16), pl.ds(0, rope)]

    loop(groups, place)
    loop(groups // 4, place_rope)

    across = {"grp": z * 2 + 1 - y}
    up, down = {"grp": ((z + 1) % half) * 2 + y}, {"grp": ((z + half - 1) % half) * 2 + y}

    def shard_of(dz, column):
        return ((z + dz + half) % half) * 2 + column

    def ring(c, way, where):
        return (
            remote(pref_lat.at[c], pref_lat.at[c], ring_send.at[way, c], ring_recv.at[c], where),
            remote(pref_rope.at[c], pref_rope.at[c], ring_rope_send.at[way, c], ring_rope_recv.at[c], where),
        )

    def send_on(c, way, where):
        for copy in ring(c, way, where):
            copy.start()

    def arrived(c):
        for copy in ring(c, 0, up):
            copy.wait_recv()

    def sent(c, way, where):
        for copy in ring(c, way, where):
            copy.wait_send()

    other = shard_of(0, 1 - y)
    send_on(mine, 0, up)
    send_on(mine, 1, down)
    send_on(mine, 2, across)
    arrived(other)
    send_on(other, 0, up)
    send_on(other, 1, down)
    for hop in (1, 2, 3):
        for column in (0, 1):
            c = shard_of(-hop, column)
            arrived(c)
            if hop < 3 or column == 0:
                send_on(c, 0, up)
            c = shard_of(hop, column)
            arrived(c)
            if hop < 3 or column == 1:
                send_on(c, 1, down)
    for column in (0, 1):
        arrived(shard_of(4, column))

    tiles, tile = scores.shape[0], scores.shape[2]
    top[...] = jnp.full_like(top, very_negative)
    total[...] = jnp.zeros_like(total)
    out[...] = jnp.zeros_like(out)

    def score(i):
        k_lat = pref_lat[pl.ds(2 * i, 2)].reshape(tile, latent)
        k_rope = pref_rope[pl.ds(2 * i, 2)].reshape(tile, rope)
        s = (contract_last(q_lat[...], k_lat) + contract_last(q_rope[...], k_rope)) * score_scale
        scores[i] = s
        top[...] = jnp.maximum(top[...], jnp.max(s, axis=1, keepdims=True))

    loop(tiles, score)

    def weigh(i):
        e = jnp.exp(scores[i] - top[...])
        total[...] += jnp.sum(e, axis=1, keepdims=True)
        k_lat = pref_lat[pl.ds(2 * i, 2)].reshape(tile, latent)
        out[...] += jnp.dot(e.astype(jnp.bfloat16), k_lat, preferred_element_type=jnp.float32)

    loop(tiles, weigh)
    one.drain()
    two.drain()
    sent(mine, 0, up)
    sent(mine, 1, down)
    sent(mine, 2, across)
    sent(other, 0, up)
    sent(other, 1, down)
    for hop in (1, 2, 3):
        for column in (0, 1):
            if hop < 3 or column == 0:
                sent(shard_of(-hop, column), 0, up)
            if hop < 3 or column == 1:
                sent(shard_of(hop, column), 1, down)


def prefix_attention(members, q_lat, q_rope, prefix_shard, store_order, prefix_of_group):
    groups = store_order.shape[0]
    rows, latent = q_lat.shape
    rope = q_rope.shape[1]
    shard = prefix_shard.shape[0]
    lanes = latent // 4
    bf16, f32 = jnp.bfloat16, jnp.float32
    vmem, smem = pl.BlockSpec(memory_space=pltpu.VMEM), pl.BlockSpec(memory_space=pltpu.SMEM)
    dma = pltpu.SemaphoreType.DMA
    return pl.pallas_call(
        functools.partial(prefix_kernel, groups, members),
        out_shape=[
            jax.ShapeDtypeStruct((rows, latent), f32),
            jax.ShapeDtypeStruct((rows, 1), f32),
            jax.ShapeDtypeStruct((rows, 1), f32),
        ],
        in_specs=[vmem, vmem, vmem, vmem, smem, smem],
        out_specs=[vmem, vmem, vmem],
        scratch_shapes=[pltpu.VMEM((groups, 32, lanes), bf16)] * 4
        + [
            pltpu.VMEM((members, shard, latent), bf16),
            pltpu.VMEM((members, shard, rope), bf16),
            pltpu.VMEM((members // 2, rows, 2 * shard), f32),
        ]
        + [dma((groups,))] * 4
        + [dma((3, members)), dma((members,)), dma((3, members)), dma((members,))],
        compiler_params=pltpu.CompilerParams(collective_id=0, has_side_effects=True, vmem_limit_bytes=40 * MIB),
        cost_estimate=pl.CostEstimate(flops=2_300_000_000, bytes_accessed=4_000_000, transcendentals=1_000_000),
    )(q_lat, q_rope, prefix_shard[:, :latent], prefix_shard[:, latent:], store_order, prefix_of_group)


def private_kernel(
    groups,
    members,
    q_lat,
    q_rope,
    new_latent,
    private_store,
    request_source,
    private_len,
    prefix_out,
    prefix_top,
    prefix_total,
    out,
    pages_in,
    pages_out,
    keys,
    ql_in,
    qr_in,
    part_out,
    part_in,
    slots,
    pages_send,
    pages_recv,
    keys_send,
    keys_recv,
    ql_send,
    ql_recv,
    qr_send,
    qr_recv,
    part_send,
    part_recv,
):
    me, mine = lax.axis_index("rep"), lax.axis_index("grp")
    requests = request_source.shape[0]
    owned = requests // members
    latent, rope = q_lat.shape[1], q_rope.shape[1]
    lanes = latent // 4
    capacity, depth = private_store.shape[1:3]
    own_rows = q_lat.shape[0] // members
    block = own_rows // owned
    greet(groups, members)

    def query_rows(j):
        return pl.ds(pl.multiple_of(j * own_rows, own_rows), own_rows)

    pages = Exchange("rep", groups, lambda j: private_store.at[j], lambda j: pages_in.at[j], lambda j: pages_send.at[j], lambda j: pages_recv.at[j])
    ql = Exchange("grp", members, lambda j: q_lat.at[query_rows(j)], lambda j: ql_in.at[j], lambda j: ql_send.at[j], lambda j: ql_recv.at[j])
    qr = Exchange("grp", members, lambda j: q_rope.at[query_rows(j)], lambda j: qr_in.at[j], lambda j: qr_send.at[j], lambda j: qr_recv.at[j])

    def key_exchange(a):
        return Exchange(
            "grp", members, lambda j: pages_out.at[j * owned + a], lambda j: keys.at[a, j], lambda j: keys_send.at[a, j], lambda j: keys_recv.at[a, j]
        )

    def part_exchange(a):
        return Exchange(
            "grp", members, lambda j: part_out.at[a, j], lambda j: part_in.at[a, j], lambda j: part_send.at[a, j], lambda j: part_recv.at[a, j]
        )

    @pl.when(me % 2 == 0)
    def _():
        pages.start()
        ql.start()
        qr.start()

    @pl.when(me % 2 == 1)
    def _():
        ql.start()
        qr.start()
        pages.start()

    pages.own().start()
    ql.own().start()
    qr.own().start()

    def find_slot(i):
        source = request_source[i]

        def count(j, rank):
            return rank + jnp.where((request_source[j] == source) & (j < i), 1, 0)

        slots[i] = jnp.minimum(lax.fori_loop(0, requests, count, jnp.int32(0)), capacity - 1)

    loop(requests, find_slot)
    pages.finish()

    def pick(i):
        pages_out[i] = pages_in[request_source[i], slots[i]]

    loop(requests, pick)
    for a in range(owned):
        key_exchange(a).start()
        key_exchange(a).own().start()
    ql.finish()
    qr.finish()

    def attend(a):
        rows = members * block
        at = pl.ds(pl.multiple_of(a * block, block), block)
        q_l = ql_in[:, at, :].reshape(rows, latent)
        q_r = qr_in[:, at, :].reshape(rows, rope)
        k = keys[a].reshape(members * depth, keys.shape[3])
        k_lat, k_rope = k[:, :latent], k[:, latent:]
        s = (contract_last(q_l, k_lat) + contract_last(q_r, k_rope)) * score_scale
        usable = lax.broadcasted_iota(jnp.int32, s.shape, 1) < private_len[mine * owned + a]
        s = jnp.where(usable, s, very_negative)
        fresh = new_latent[mine * owned + a].astype(jnp.float32)
        q_l32, q_r32 = q_l.astype(jnp.float32), q_r.astype(jnp.float32)
        step = (lax.broadcasted_iota(jnp.int32, (rows, 1), 0) % block) // (block // 2)
        new_s = []
        for u in range(2):
            row = fresh[u : u + 1]
            s_u = (
                jnp.sum(q_l32 * row[:, :latent], axis=1, keepdims=True) + jnp.sum(q_r32 * row[:, latent:], axis=1, keepdims=True)
            ) * score_scale
            new_s.append(jnp.where(step >= u, s_u, very_negative))
        m = jnp.maximum(jnp.max(s, axis=1, keepdims=True), jnp.maximum(new_s[0], new_s[1]))
        e = jnp.where(usable, jnp.exp(s - m), 0.0)
        length = jnp.sum(e, axis=1, keepdims=True)
        weighted = jnp.dot(e.astype(jnp.bfloat16), k_lat, preferred_element_type=jnp.float32)
        for u in range(2):
            e_u = jnp.where(step >= u, jnp.exp(new_s[u] - m), 0.0)
            length = length + e_u
            weighted = weighted + e_u.astype(jnp.bfloat16).astype(jnp.float32) * fresh[u : u + 1, :latent]
        lse = m + jnp.log(length)
        high = lse.astype(jnp.bfloat16).astype(jnp.float32)
        middle = (lse - high).astype(jnp.bfloat16).astype(jnp.float32)
        low = lse - high - middle
        place = lax.broadcasted_iota(jnp.int32, (rows, lanes), 1)
        tail = jnp.where(place == 0, high, jnp.where(place == 1, middle, jnp.where(place == 2, low, 0.0)))
        part_out[a, :, :, pl.ds(0, latent)] = (weighted / length).astype(jnp.bfloat16).reshape(members, block, latent)
        part_out[a, :, :, pl.ds(latent, lanes)] = tail.astype(jnp.bfloat16).reshape(members, block, lanes)

    def attend_and_send(a):
        key_exchange(a).finish()
        attend(a)
        part_exchange(a).start()
        part_exchange(a).own().start()

    loop(owned, attend_and_send)

    def merge(a, j):
        rows = pl.ds(pl.multiple_of(j * own_rows + a * block, block), block)
        tail = part_in[a, j, :, pl.ds(latent, lanes)].astype(jnp.float32)
        lse = jnp.sum(tail, axis=1, keepdims=True)
        part = part_in[a, j, :, pl.ds(0, latent)].astype(jnp.float32)
        top = prefix_top[rows]
        m = jnp.maximum(top, lse)
        scale, part_scale = jnp.exp(top - m), jnp.exp(lse - m)
        length = prefix_total[rows] * scale + part_scale
        out[rows] = ((prefix_out[rows] * scale + part * part_scale) / length).astype(jnp.bfloat16)

    def merge_all(a):
        part_exchange(a).finish()
        loop(members, lambda j: merge(a, j))

    loop(owned, merge_all)
    pages.drain()
    ql.drain()
    qr.drain()
    for a in range(owned):
        key_exchange(a).drain()
        part_exchange(a).drain()


def private_attention(members, q_lat, q_rope, new_latent, private_store, request_source, private_len, prefix_out, prefix_top, prefix_total):
    groups, capacity, depth, width = private_store.shape
    rows, latent = q_lat.shape
    rope = q_rope.shape[1]
    requests = new_latent.shape[0]
    owned = requests // members
    own = rows // members
    lanes = latent // 4
    bf16 = jnp.bfloat16
    vmem, smem, anywhere = [pl.BlockSpec(memory_space=m) for m in (pltpu.VMEM, pltpu.SMEM, pl.ANY)]
    dma = pltpu.SemaphoreType.DMA
    return pl.pallas_call(
        functools.partial(private_kernel, groups, members),
        out_shape=jax.ShapeDtypeStruct((rows, latent), bf16),
        in_specs=[vmem, vmem, vmem, anywhere, smem, smem, vmem, vmem, vmem],
        out_specs=vmem,
        scratch_shapes=[
            pltpu.VMEM((groups, capacity, depth, width), bf16),
            pltpu.VMEM((requests, depth, width), bf16),
            pltpu.VMEM((owned, members, depth, width), bf16),
            pltpu.VMEM((members, own, latent), bf16),
            pltpu.VMEM((members, own, rope), bf16),
            pltpu.VMEM((owned, members, own // owned, latent + lanes), bf16),
            pltpu.VMEM((owned, members, own // owned, latent + lanes), bf16),
            pltpu.SMEM((requests,), jnp.int32),
            dma((groups,)),
            dma((groups,)),
            dma((owned, members)),
            dma((owned, members)),
            dma((members,)),
            dma((members,)),
            dma((members,)),
            dma((members,)),
            dma((owned, members)),
            dma((owned, members)),
        ],
        compiler_params=pltpu.CompilerParams(collective_id=1, has_side_effects=True, vmem_limit_bytes=40 * MIB),
        cost_estimate=pl.CostEstimate(flops=400_000_000, bytes_accessed=8_000_000, transcendentals=1_000_000),
    )(q_lat, q_rope, new_latent, private_store, request_source, private_len, prefix_out, prefix_top, prefix_total)


def shards(
    members,
    q_nope,
    q_rope,
    new_latent,
    w_uk,
    w_uv,
    prefix_store,
    store_order,
    prefix_of_group,
    private_store,
    request_source,
    private_len,
):
    requests, steps, heads = q_nope.shape[:3]
    rows = requests * steps * heads
    q_lat = jnp.einsum("rthn,hnc->rthc", q_nope, w_uk, preferred_element_type=jnp.float32).astype(jnp.bfloat16)
    q_lat, q_rope = q_lat.reshape(rows, -1), q_rope.reshape(rows, -1)
    prefix = prefix_attention(members, q_lat, q_rope, prefix_store[0], store_order, prefix_of_group)
    attended = private_attention(members, q_lat, q_rope, new_latent, private_store[0], request_source[:, 0], private_len[0], *prefix)
    attended = attended.reshape(requests, steps, heads, -1)
    return jnp.einsum("rthc,hcv->rthv", attended, w_uv, preferred_element_type=jnp.float32).astype(jnp.bfloat16)


def solution(mesh):
    in_specs = (
        P("rep", None, "grp", None),
        P("rep", None, "grp", None),
        P("rep", None, None),
        P("grp", None, None),
        P("grp", None, None),
        P("rep", "grp", None),
        P(),
        P(),
        P("rep", None, None, "grp", None),
        P("rep", None),
        P("rep", None),
    )
    out_specs = P("rep", None, "grp", None)
    body = functools.partial(shards, mesh.shape["grp"])
    return jax.shard_map(body, mesh=mesh, in_specs=in_specs, out_specs=out_specs, check_vma=False)
```

time: 216 us -> 165 us (0.76)
  Pallas kernels: 0 us -> 160 us
  waiting for transfers between devices: 89.6 us -> 0 us
  blocking collectives: 45.7 us -> 0 us
  starting transfers between devices: 30.6 us -> 0 us
  between operations: 13.7 us -> 0.15 us
  matrix products: 14.7 us -> 1.94 us
  other arithmetic: 9.19 us -> 0 us
  local copies, waits for them, and re-layouts: 11.5 us -> 2.37 us
    pallas_call x0 -> x2, Pallas kernels: none -> 160 us  [the longest x1 85 us: private_attention(): pl.pallas_call(functools.partial(private_kernel, groups, members), out_sh...]
    all_to_all x4 -> x0, waiting for transfers between devices: 76 us -> none  [the longest x1 32.4 us: shards(): lax.all_to_all(private_store, 'rep', split_axis=1, concat_axis=0, tiled=T...]
    all_to_all x2 -> x0, blocking collectives: 45.7 us -> none  [the longest x1 31 us: shards(): back = lax.all_to_all(back, 'grp', split_axis=2, concat_axis=0, tiled=True)]
    all_to_all x4 -> x0, starting transfers between devices: 30.5 us -> none  [the longest x1 11.1 us: shards(): q_owned = lax.all_to_all(q, 'grp', split_axis=0, concat_axis=2, tiled=True)]
    dot_general x6 -> x1, matrix products: 14.4 us -> 0.71 us  [shards(): jnp.einsum('rthc,hcv->rthv', attended, w_uv, preferred_element_type=jnp.f...]
    all_gather x1 -> x0, waiting for transfers between devices: 13.6 us -> none  [shards(): shared = lax.all_gather(shard, 'grp', axis=0, tiled=True)]
    reduce_sum x5 -> x0, other arithmetic: 5.04 us -> none  [the longest x1 4.36 us: shards(): total = jnp.sum(e, axis=-1)]
    all_to_all x3 -> x0, other arithmetic: 3.11 us -> none  [the longest x2 1.58 us: spread_prefix(): lax.all_to_all(chosen, 'rep', split_axis=0, concat_axis=0, tiled=True)]
  transfers between devices with their start and end apart: 5 -> 0, of which waited for: 5 -> 0; matrix products, arithmetic and copies ran while one was open for 6% -> 0% of each run, Pallas kernels for 0% -> 0%
where the time goes in v2:
time: 165 us; the launch traced here: 164 us
  Pallas kernels  160 us (97%)
  local copies, waits for them, and re-layouts  2.37 us (1%)
  matrix products  1.94 us (1%)
    pallas_call x1, Pallas kernels, private_attention(): pl.pallas_call(functools.partial(private_kernel, groups, members), out_sh...  85 us
    pallas_call x1, Pallas kernels, prefix_attention(): pl.pallas_call(functools.partial(prefix_kernel, groups, members), out_sha...  74.6 us

profile of v2, /device:TPU:6, one launch (start us, length us, event | category | flops | bytes accessed | tf_op | source)
XLA Modules:
  0.0 164.1 jit_solution(7935176573618057943)
XLA Ops:
  0.0 0.0 copy-start
  0.0 1.1 copy.14
  1.2 0.1 copy-done
  1.3 0.0 copy-start.2
  1.3 0.0 copy-start.6
  1.3 0.0 copy-start.7
  1.3 1.2 fusion
  2.5 0.3 copy.13
  2.8 0.0 copy-done.2
  2.9 0.0 copy-done.6
  2.9 0.0 copy-done.7
  2.9 0.0 copy-start.1
  2.9 0.0 copy-start.3
  2.9 0.0 copy-start.4
  2.9 0.0 copy-start.5
  2.9 74.6 %shard_map.109 = (f32[512,512]{1,0:T(8,128)S(1)}, f32[512,1]{1,0:T(8,128)S(1)}, f32[512,1]{1,0:T(8,128)S(1)}) custom-call(bf16[512,512]{1,0:T(8,128)(2,1)S(1)} %bitcast.21, bf16[512,64]{1,0:T(8,128)(2,1)S(1)} %bitcast.25, bf16[128,512]{1,0:T(8,128)(2,1)S(1)} %slice.8.store_lat, bf16[128,64]{1,0:T(8,128)(2,1)S(1)} %slice.9.store_rope, s32[32]{0:T(128)S(1)} %copy-done.6, ...), custom_call_target="tpu_custom_call" | custom-call | flops 2300000000 | bytes 4000000 | tf_op jit(solution)/shard_map/pallas_call | solution.py:235
  77.6 0.0 copy-done.1
  77.6 0.0 copy-done.3
  77.6 0.0 copy-done.4
  77.6 0.0 copy-done.5
  77.6 0.0 copy-start.8
  77.6 85.0 %shard_map.110 = bf16[512,512]{1,0:T(8,128)(2,1)S(1)} custom-call(bf16[512,512]{1,0:T(8,128)(2,1)S(1)} %bitcast.22, bf16[512,64]{1,0:T(8,128)(2,1)S(1)} %bitcast.26, bf16[32,2,576]{2,1,0:T(2,128)(2,1)S(1)} %copy-done.3, bf16[32,2,16,576]{3,2,1,0:T(8,128)(2,1)S(1)} %bitcast.24, s32[32]{0:T(128)S(1)} %bitcast.27, s32[32]{0:T(128)S(1)} %bitcast.28, ...), custom_call_target="tpu_custom_call" | custom-call | flops 400000000 | bytes 8000000 | tf_op jit(solution)/shard_map/pallas_call | solution.py:433
  162.6 0.0 copy-done.8
  162.6 0.7 fusion.1
  163.3 0.8 copy.16
  (2 shorter events, 0.0 us)
Async XLA Ops:
  0.0 1.3 copy-start
  1.3 1.5 copy-start.2
  1.3 1.6 copy-start.6
  1.3 1.6 copy-start.7
  2.9 74.7 %copy-start.1 = (bf16[1,32,2,16,576]{4,3,2,1,0:T(8,128)(2,1)S(1)}, bf16[1,32,2,16,576]{4,3,2,1,0:T(8,128)(2,1)}, u32[]{:S(2)}) copy-start(bf16[1,32,2,16,576]{4,3,2,1,0:T(8,128)(2,1)} %param.19) | copy-start | bytes 3538948
  2.9 74.7 %copy-start.3 = (bf16[32,2,576]{2,1,0:T(2,128)(2,1)S(1)}, bf16[32,2,576]{2,1,0:T(2,128)(2,1)}, u32[]{:S(2)}) copy-start(bf16[32,2,576]{2,1,0:T(2,128)(2,1)} %new_latent.1) | copy-start | bytes 221188
  2.9 74.7 %copy-start.4 = (s32[32,1]{0,1:T(1,128)S(1)}, s32[32,1]{0,1:T(1,128)}, u32[]{:S(2)}) copy-start(s32[32,1]{0,1:T(1,128)} %param.20) | copy-start | bytes 388
  2.9 74.7 %copy-start.5 = (s32[1,32]{1,0:T(1,128)S(1)}, s32[1,32]{1,0:T(1,128)}, u32[]{:S(2)}) copy-start(s32[1,32]{1,0:T(1,128)} %param.21) | copy-start | bytes 388
  77.6 85.0 %copy-start.8 = (bf16[8,512,128]{2,1,0:T(8,128)(2,1)S(1)}, bf16[8,512,128]{2,1,0:T(8,128)(2,1)}, u32[]{:S(2)}) copy-start(bf16[8,512,128]{2,1,0:T(8,128)(2,1)} %param.15) | copy-start | bytes 3145732

commit v3 on v2

v3 whole, which is shorter than its diff:
```python
import functools

import jax
import jax.numpy as jnp
from jax import lax
from jax.experimental import pallas as pl
from jax.experimental.pallas import tpu as pltpu
from jax.sharding import PartitionSpec as P

score_scale = 192.0 ** (-0.5)
very_negative = -1e30
MIB = 1024 * 1024
MESH = pl.DeviceIdType.MESH
EARLY = 12
ATTEND_AFTER = 3


def contract_last(a, b):
    return lax.dot_general(a, b, (((1,), (1,)), ((), ())), preferred_element_type=jnp.float32)


def loop(count, body):
    def step(i, carry):
        body(i)
        return carry

    lax.fori_loop(0, count, step, 0)


def remote(src, dst, send, recv, where):
    return pltpu.make_async_remote_copy(
        src_ref=src, dst_ref=dst, send_sem=send, recv_sem=recv, device_id=where, device_id_type=MESH
    )


def greet(groups, members):
    me, mine = lax.axis_index("rep"), lax.axis_index("grp")
    barrier = pltpu.get_barrier_semaphore()

    def along_rep(k):
        pl.semaphore_signal(barrier, inc=1, device_id={"rep": (me + k + 1) % groups}, device_id_type=MESH)

    def along_grp(k):
        pl.semaphore_signal(barrier, inc=1, device_id={"grp": (mine + k + 1) % members}, device_id_type=MESH)

    loop(groups - 1, along_rep)
    loop(members - 1, along_grp)
    pl.semaphore_wait(barrier, groups + members - 2)


class Exchange:
    def __init__(self, axis, peers, out_ref, in_ref, send, recv):
        self.axis, self.peers, self.out_ref, self.in_ref, self.send, self.recv = axis, peers, out_ref, in_ref, send, recv
        self.me = lax.axis_index(axis)

    def peer(self, k):
        return (self.me + k + 1) % self.peers

    def to(self, j):
        return remote(self.out_ref(j), self.in_ref(self.me), self.send(j), self.recv(self.me), {self.axis: j})

    def own(self):
        return pltpu.make_async_copy(self.out_ref(self.me), self.in_ref(self.me), self.recv(self.me))

    def start(self, begin=0, end=None):
        loop((self.peers - 1 if end is None else end) - begin, lambda k: self.to(self.peer(k + begin)).start())

    def arrive(self, j):
        remote(self.out_ref(j), self.in_ref(j), self.send(j), self.recv(j), {self.axis: j}).wait_recv()

    def finish(self):
        self.own().wait()
        loop(self.peers - 1, lambda k: self.arrive(self.peer(k)))

    def drain(self):
        loop(self.peers - 1, lambda k: self.to(self.peer(k)).wait_send())


def kernel(
    groups,
    members,
    q_lat,
    q_rope,
    new_latent,
    store_lat,
    store_rope,
    store_order,
    prefix_of_group,
    private_store,
    request_source,
    private_len,
    out,
    q_out,
    q_in,
    one_out,
    one_in,
    two_out,
    two_in,
    pref,
    scores,
    weighted,
    top,
    total,
    pages_in,
    pages_out,
    keys,
    part_out,
    part_in,
    slots,
    one_send,
    one_recv,
    two_send,
    two_recv,
    ring_send,
    ring_recv,
    pages_send,
    pages_recv,
    keys_send,
    keys_recv,
    q_send,
    q_recv,
    part_send,
    part_recv,
):
    me, mine = lax.axis_index("rep"), lax.axis_index("grp")
    half = members // 2
    z, y = mine // 2, mine % 2
    latent, rope = q_lat.shape[1], q_rope.shape[1]
    lanes = latent // 4
    requests = request_source.shape[0]
    owned = requests // members
    capacity, depth = private_store.shape[1:3]
    own_rows = q_lat.shape[0] // members
    block = own_rows // owned

    def rows_of(j):
        return pl.ds(pl.multiple_of((j // 4) * 16, 16), 16)

    def columns_of(j):
        return pl.ds(pl.multiple_of((j % 4) * lanes, lanes), lanes)

    def cut(j):
        one_out[j, pl.ds(0, 16)] = store_lat[rows_of(j), columns_of(j)]
        one_out[j, pl.ds(16, 16)] = jnp.concatenate([store_rope[rows_of(j)], jnp.zeros((16, lanes - rope), jnp.bfloat16)], axis=1)

    loop(groups, cut)

    def query_rows(j):
        return pl.ds(pl.multiple_of(j * own_rows, own_rows), own_rows)

    def put_query(j):
        q_out[j, :, pl.ds(0, latent)] = q_lat[query_rows(j)]
        q_out[j, :, pl.ds(latent, lanes)] = jnp.concatenate(
            [q_rope[query_rows(j)], jnp.zeros((own_rows, lanes - rope), jnp.bfloat16)], axis=1
        )

    loop(members, put_query)
    greet(groups, members)
    one = Exchange("rep", groups, lambda j: one_out.at[j], lambda j: one_in.at[j], lambda j: one_send.at[j], lambda j: one_recv.at[j])
    two = Exchange("rep", groups, lambda j: two_out.at[j], lambda j: two_in.at[j], lambda j: two_send.at[j], lambda j: two_recv.at[j])
    pages = Exchange("rep", groups, lambda j: private_store.at[j], lambda j: pages_in.at[j], lambda j: pages_send.at[j], lambda j: pages_recv.at[j])
    queries = Exchange("grp", members, lambda j: q_out.at[j], lambda j: q_in.at[j], lambda j: q_send.at[j], lambda j: q_recv.at[j])

    def key_exchange(a):
        return Exchange(
            "grp", members, lambda j: pages_out.at[j * owned + a], lambda j: keys.at[a, j], lambda j: keys_send.at[a, j], lambda j: keys_recv.at[a, j]
        )

    def part_exchange(a):
        return Exchange(
            "grp", members, lambda j: part_out.at[a, j], lambda j: part_in.at[a, j], lambda j: part_send.at[a, j], lambda j: part_recv.at[a, j]
        )

    one.start()
    one.own().start()

    @pl.when(me % 2 == 1)
    def _():
        queries.start()

    pages.start(0, EARLY)
    pages.own().start()
    queries.own().start()
    one.finish()

    def choose(j):
        two_out[j] = one_in[store_order[prefix_of_group[j]]]

    loop(groups, choose)
    two.start()
    two.own().start()
    pages.start(EARLY, groups - 1)

    @pl.when(me % 2 == 0)
    def _():
        queries.start()


    def find_slot(i):
        source = request_source[i]

        def count(j, rank):
            return rank + jnp.where((request_source[j] == source) & (j < i), 1, 0)

        slots[i] = jnp.minimum(lax.fori_loop(0, requests, count, jnp.int32(0)), capacity - 1)

    loop(requests, find_slot)
    pages.finish()

    def pick(i):
        pages_out[i] = pages_in[request_source[i], slots[i]]

    loop(requests, pick)
    for a in range(owned):
        key_exchange(a).start()
        key_exchange(a).own().start()
    two.finish()

    def place(j):
        pref[mine, rows_of(j), columns_of(j)] = two_in[j, pl.ds(0, 16)]

    def place_rope(b):
        pref[mine, pl.ds(pl.multiple_of(b * 16, 16), 16), pl.ds(latent, lanes)] = two_in[4 * b, pl.ds(16, 16)]

    loop(groups, place)
    loop(groups // 4, place_rope)

    across = {"grp": z * 2 + 1 - y}
    up, down = {"grp": ((z + 1) % half) * 2 + y}, {"grp": ((z + half - 1) % half) * 2 + y}

    def shard_of(dz, column):
        return ((z + dz + half) % half) * 2 + column

    def ring(c, way, where):
        return remote(pref.at[c], pref.at[c], ring_send.at[way, c], ring_recv.at[c], where)

    def arrived(c):
        ring(c, 0, up).wait_recv()

    sends = []

    def send_on(c, way, where):
        ring(c, way, where).start()
        sends.append((c, way, where))

    other = shard_of(0, 1 - y)
    send_on(mine, 0, up)
    send_on(mine, 1, down)
    send_on(mine, 2, across)
    width = pref.shape[2]

    def attend(a):
        rows = members * block
        at = pl.ds(pl.multiple_of(a * block, block), block)
        q = q_in[:, at, :].reshape(rows, width)[:, : latent + rope]
        k = keys[a].reshape(members * depth, latent + rope)
        s = contract_last(q, k) * score_scale
        usable = lax.broadcasted_iota(jnp.int32, s.shape, 1) < private_len[mine * owned + a]
        s = jnp.where(usable, s, very_negative)
        fresh = new_latent[mine * owned + a].astype(jnp.float32)
        q32 = q.astype(jnp.float32)
        step = (lax.broadcasted_iota(jnp.int32, (rows, 1), 0) % block) // (block // 2)
        new_s = []
        for u in range(2):
            s_u = jnp.sum(q32 * fresh[u : u + 1], axis=1, keepdims=True) * score_scale
            new_s.append(jnp.where(step >= u, s_u, very_negative))
        m = jnp.maximum(jnp.max(s, axis=1, keepdims=True), jnp.maximum(new_s[0], new_s[1]))
        e = jnp.where(usable, jnp.exp(s - m), 0.0)
        length = jnp.sum(e, axis=1, keepdims=True)
        summed = jnp.dot(e.astype(jnp.bfloat16), k[:, :latent], preferred_element_type=jnp.float32)
        for u in range(2):
            e_u = jnp.where(step >= u, jnp.exp(new_s[u] - m), 0.0)
            length = length + e_u
            summed = summed + e_u.astype(jnp.bfloat16).astype(jnp.float32) * fresh[u : u + 1, :latent]
        lse = m + jnp.log(length)
        high = lse.astype(jnp.bfloat16).astype(jnp.float32)
        middle = (lse - high).astype(jnp.bfloat16).astype(jnp.float32)
        low = lse - high - middle
        place = lax.broadcasted_iota(jnp.int32, (rows, lanes), 1)
        tail = jnp.where(place == 0, high, jnp.where(place == 1, middle, jnp.where(place == 2, low, 0.0)))
        part_out[a, :, :, pl.ds(0, latent)] = (summed / length).astype(jnp.bfloat16).reshape(members, block, latent)
        part_out[a, :, :, pl.ds(latent, lanes)] = tail.astype(jnp.bfloat16).reshape(members, block, lanes)

    def attend_and_send(a):
        key_exchange(a).finish()
        attend(a)
        part_exchange(a).start()
        part_exchange(a).own().start()

    tile = scores.shape[2]
    rows = q_lat.shape[0]
    top[...] = jnp.full_like(top, very_negative)
    total[...] = jnp.zeros_like(total)
    weighted[...] = jnp.zeros_like(weighted)

    def score(i):
        k = pref[pl.ds(2 * i, 2)].reshape(tile, width)
        s = contract_last(q_out[...].reshape(rows, width), k) * score_scale
        scores[i] = s
        top[...] = jnp.maximum(top[...], jnp.max(s, axis=1, keepdims=True))

    def attend_at(hop):
        if hop == ATTEND_AFTER:
            queries.finish()
            loop(owned, attend_and_send)

    arrived(other)
    send_on(other, 0, up)
    send_on(other, 1, down)
    attend_at(0)
    for hop in (1, 2, 3):
        for column in (0, 1):
            c = shard_of(-hop, column)
            arrived(c)
            if hop < 3 or column == 0:
                send_on(c, 0, up)
            c = shard_of(hop, column)
            arrived(c)
            if hop < 3 or column == 1:
                send_on(c, 1, down)
        attend_at(hop)
    for column in (0, 1):
        arrived(shard_of(4, column))
    loop(half, score)

    def weigh(i):
        e = jnp.exp(scores[i] - top[...])
        total[...] += jnp.sum(e, axis=1, keepdims=True)
        k = pref[pl.ds(2 * i, 2), :, pl.ds(0, latent)].reshape(tile, latent)
        weighted[...] += jnp.dot(e.astype(jnp.bfloat16), k, preferred_element_type=jnp.float32)

    loop(half, weigh)

    def merge(a, j):
        at = pl.ds(pl.multiple_of(j * own_rows + a * block, block), block)
        tail = part_in[a, j, :, pl.ds(latent, lanes)].astype(jnp.float32)
        lse = jnp.sum(tail, axis=1, keepdims=True)
        part = part_in[a, j, :, pl.ds(0, latent)].astype(jnp.float32)
        m = jnp.maximum(top[at], lse)
        scale, part_scale = jnp.exp(top[at] - m), jnp.exp(lse - m)
        share = 1.0 / (total[at] * scale + part_scale)
        out[at] = (weighted[at] * (scale * share) + part * (part_scale * share)).astype(jnp.bfloat16)

    def merge_all(a):
        part_exchange(a).finish()

        def four(i):
            for j in range(4):
                merge(a, 4 * i + j)

        loop(members // 4, four)

    loop(owned, merge_all)
    for exchange in [one, two, pages, queries] + [f(a) for a in range(owned) for f in (key_exchange, part_exchange)]:
        exchange.drain()
    for c, way, where in sends:
        ring(c, way, where).wait_send()


def attention(members, q_lat, q_rope, new_latent, prefix_shard, store_order, prefix_of_group, private_store, request_source, private_len):
    groups, capacity, depth, width = private_store.shape
    rows, latent = q_lat.shape
    rope = q_rope.shape[1]
    requests = new_latent.shape[0]
    owned = requests // members
    own = rows // members
    shard = prefix_shard.shape[0]
    lanes = latent // 4
    wide = latent + lanes
    bf16, f32 = jnp.bfloat16, jnp.float32
    vmem, smem, anywhere = [pl.BlockSpec(memory_space=m) for m in (pltpu.VMEM, pltpu.SMEM, pl.ANY)]
    dma = pltpu.SemaphoreType.DMA
    return pl.pallas_call(
        functools.partial(kernel, groups, members),
        out_shape=jax.ShapeDtypeStruct((rows, latent), bf16),
        in_specs=[vmem, vmem, vmem, vmem, vmem, smem, smem, anywhere, smem, smem],
        out_specs=vmem,
        scratch_shapes=[pltpu.VMEM((members, own, wide), bf16)] * 2
        + [pltpu.VMEM((groups, 32, lanes), bf16)] * 4
        + [
            pltpu.VMEM((members, shard, wide), bf16),
            pltpu.VMEM((members // 2, rows, 2 * shard), f32),
            pltpu.VMEM((rows, latent), f32),
            pltpu.VMEM((rows, 1), f32),
            pltpu.VMEM((rows, 1), f32),
            pltpu.VMEM((groups, capacity, depth, width), bf16),
            pltpu.VMEM((requests, depth, width), bf16),
            pltpu.VMEM((owned, members, depth, width), bf16),
            pltpu.VMEM((owned, members, own // owned, wide), bf16),
            pltpu.VMEM((owned, members, own // owned, wide), bf16),
            pltpu.SMEM((requests,), jnp.int32),
        ]
        + [dma((groups,))] * 4
        + [dma((3, members)), dma((members,))]
        + [dma((groups,))] * 2
        + [dma((owned, members))] * 2
        + [dma((members,))] * 2
        + [dma((owned, members))] * 2,
        compiler_params=pltpu.CompilerParams(collective_id=0, has_side_effects=True, vmem_limit_bytes=40 * MIB),
        cost_estimate=pl.CostEstimate(flops=2_700_000_000, bytes_accessed=8_000_000, transcendentals=2_000_000),
    )(
        q_lat,
        q_rope,
        new_latent,
        prefix_shard[:, :latent],
        prefix_shard[:, latent:],
        store_order,
        prefix_of_group,
        private_store,
        request_source,
        private_len,
    )


def shards(
    members,
    q_nope,
    q_rope,
    new_latent,
    w_uk,
    w_uv,
    prefix_store,
    store_order,
    prefix_of_group,
    private_store,
    request_source,
    private_len,
):
    requests, steps, heads = q_nope.shape[:3]
    rows = requests * steps * heads
    q_lat = jnp.einsum("rthn,hnc->rthc", q_nope, w_uk, preferred_element_type=jnp.float32).astype(jnp.bfloat16)
    q_lat, q_rope = q_lat.reshape(rows, -1), q_rope.reshape(rows, -1)
    attended = attention(
        members,
        q_lat,
        q_rope,
        new_latent,
        prefix_store[0],
        store_order,
        prefix_of_group,
        private_store[0],
        request_source[:, 0],
        private_len[0],
    )
    attended = attended.reshape(requests, steps, heads, -1)
    return jnp.einsum("rthc,hcv->rthv", attended, w_uv, preferred_element_type=jnp.float32).astype(jnp.bfloat16)


def solution(mesh):
    in_specs = (
        P("rep", None, "grp", None),
        P("rep", None, "grp", None),
        P("rep", None, None),
        P("grp", None, None),
        P("grp", None, None),
        P("rep", "grp", None),
        P(),
        P(),
        P("rep", None, None, "grp", None),
        P("rep", None),
        P("rep", None),
    )
    out_specs = P("rep", None, "grp", None)
    body = functools.partial(shards, mesh.shape["grp"])
    return jax.shard_map(body, mesh=mesh, in_specs=in_specs, out_specs=out_specs, check_vma=False)
```

time: 165 us -> 137 us (0.83)
  the two profiles are of different devices: /device:TPU:6 before, /device:TPU:30 now
where the time goes in v3:
time: 137 us
  Pallas kernels  133 us (97%)
  local copies, waits for them, and re-layouts  2.37 us (2%)
  matrix products  2.02 us (1%)
    pallas_call x1, Pallas kernels, attention(): pl.pallas_call(functools.partial(kernel, groups, members), out_shape=jax....  133 us

profile of v3, /device:TPU:30, one launch (start us, length us, event | category | flops | bytes accessed | tf_op | source)
XLA Modules:
  0.0 137.0 jit_solution(7341801748278178269)
XLA Ops:
  0.0 0.0 copy-start
  0.0 1.1 copy.14
  1.2 0.1 copy-done
  1.3 0.0 copy-start.1
  1.3 0.0 copy-start.2
  1.3 0.0 copy-start.3
  1.3 0.0 copy-start.4
  1.3 0.0 copy-start.5
  1.3 0.0 copy-start.6
  1.3 0.0 copy-start.7
  1.3 1.3 fusion
  2.7 0.3 copy.13
  3.0 0.0 copy-done.1
  3.0 0.0 copy-done.2
  3.0 0.0 copy-done.3
  3.0 0.0 copy-done.4
  3.0 0.0 copy-done.5
  3.0 0.0 copy-done.6
  3.0 0.0 copy-done.7
  3.0 0.0 copy-start.8
  3.0 132.5 %shard_map.109 = bf16[512,512]{1,0:T(8,128)(2,1)S(1)} custom-call(bf16[512,512]{1,0:T(8,128)(2,1)S(1)} %bitcast.21, bf16[512,64]{1,0:T(8,128)(2,1)S(1)} %bitcast.24, bf16[32,2,576]{2,1,0:T(2,128)(2,1)S(1)} %copy-done.3, bf16[128,512]{1,0:T(8,128)(2,1)S(1)} %slice.8.store_lat, bf16[128,64]{1,0:T(8,128)(2,1)S(1)} %slice.9.store_rope, s32[32]{0:T(128)S(1)} %copy-done.4, ...), custom_call_target="tpu_custom_call" | custom-call | flops 2700000000 | bytes 8000000 | tf_op jit(solution)/shard_map/pallas_call | solution.py:373
  135.6 0.0 copy-done.8
  135.6 0.7 fusion.1
  136.3 0.8 copy.16
  (2 shorter events, 0.0 us)
Async XLA Ops:
  0.0 1.3 copy-start
  1.3 1.7 %copy-start.1 = (bf16[1,32,2,16,576]{4,3,2,1,0:T(8,128)(2,1)S(1)}, bf16[1,32,2,16,576]{4,3,2,1,0:T(8,128)(2,1)}, u32[]{:S(2)}) copy-start(bf16[1,32,2,16,576]{4,3,2,1,0:T(8,128)(2,1)} %param.19) | copy-start | bytes 3538948
  1.3 1.7 %copy-start.2 = (bf16[32,2,8,64]{3,2,1,0:T(8,128)(2,1)S(1)}, bf16[32,2,8,64]{3,2,1,0:T(8,128)(2,1)}, u32[]{:S(2)}) copy-start(bf16[32,2,8,64]{3,2,1,0:T(8,128)(2,1)} %param.12) | copy-start | bytes 196612
  1.3 1.7 %copy-start.3 = (bf16[32,2,576]{2,1,0:T(2,128)(2,1)S(1)}, bf16[32,2,576]{2,1,0:T(2,128)(2,1)}, u32[]{:S(2)}) copy-start(bf16[32,2,576]{2,1,0:T(2,128)(2,1)} %new_latent.1) | copy-start | bytes 221188
  1.3 1.7 %copy-start.4 = (s32[32]{0:T(128)S(1)}, s32[32]{0:T(128)}, u32[]{:S(2)}) copy-start(s32[32]{0:T(128)} %store_order.1) | copy-start | bytes 388
  1.3 1.7 %copy-start.5 = (s32[32]{0:T(128)S(1)}, s32[32]{0:T(128)}, u32[]{:S(2)}) copy-start(s32[32]{0:T(128)} %prefix_of_group.1) | copy-start | bytes 388
  1.3 1.7 %copy-start.6 = (s32[32,1]{0,1:T(1,128)S(1)}, s32[32,1]{0,1:T(1,128)}, u32[]{:S(2)}) copy-start(s32[32,1]{0,1:T(1,128)} %param.20) | copy-start | bytes 388
  1.3 1.7 %copy-start.7 = (s32[1,32]{1,0:T(1,128)S(1)}, s32[1,32]{1,0:T(1,128)}, u32[]{:S(2)}) copy-start(s32[1,32]{1,0:T(1,128)} %param.21) | copy-start | bytes 388
  3.0 132.5 %copy-start.8 = (bf16[8,512,128]{2,1,0:T(8,128)(2,1)S(1)}, bf16[8,512,128]{2,1,0:T(8,128)(2,1)}, u32[]{:S(2)}) copy-start(bf16[8,512,128]{2,1,0:T(8,128)(2,1)} %param.15) | copy-start | bytes 3145732

commit v4 on v3

--- a/solution.py
+++ b/solution.py
@@ -12,7 +12,7 @@
 MIB = 1024 * 1024
 MESH = pl.DeviceIdType.MESH
 EARLY = 12
-ATTEND_AFTER = 3
+ODD_PAGES = 1
 
 
 def contract_last(a, b):
@@ -82,8 +82,7 @@
     q_lat,
     q_rope,
     new_latent,
-    store_lat,
-    store_rope,
+    prefix_shard,
     store_order,
     prefix_of_group,
     private_store,
@@ -102,10 +101,14 @@
     top,
     total,
     pages_in,
-    pages_out,
-    keys,
-    part_out,
-    part_in,
+    pages_out0,
+    pages_out1,
+    keys0,
+    keys1,
+    part_out0,
+    part_out1,
+    part_in0,
+    part_in1,
     slots,
     one_send,
     one_recv,
@@ -132,6 +135,7 @@
     capacity, depth = private_store.shape[1:3]
     own_rows = q_lat.shape[0] // members
     block = own_rows // owned
+    shard = prefix_shard.shape[0]
 
     def rows_of(j):
         return pl.ds(pl.multiple_of((j // 4) * 16, 16), 16)
@@ -140,10 +144,14 @@
         return pl.ds(pl.multiple_of((j % 4) * lanes, lanes), lanes)
 
     def cut(j):
-        one_out[j, pl.ds(0, 16)] = store_lat[rows_of(j), columns_of(j)]
-        one_out[j, pl.ds(16, 16)] = jnp.concatenate([store_rope[rows_of(j)], jnp.zeros((16, lanes - rope), jnp.bfloat16)], axis=1)
+        one_out[j, pl.ds(0, 16)] = prefix_shard[rows_of(j), columns_of(j)]
+
+    def cut_rope(j):
+        sides = [prefix_shard[pl.ds(pl.multiple_of((j % 4) * 32 + 16 * side, 16), 16), pl.ds(latent, rope)] for side in (0, 1)]
+        one_out[j, pl.ds(16, 16)] = jnp.concatenate(sides, axis=1)
 
     loop(groups, cut)
+    loop(groups, cut_rope)
 
     def query_rows(j):
         return pl.ds(pl.multiple_of(j * own_rows, own_rows), own_rows)
@@ -161,15 +169,14 @@
     pages = Exchange("rep", groups, lambda j: private_store.at[j], lambda j: pages_in.at[j], lambda j: pages_send.at[j], lambda j: pages_recv.at[j])
     queries = Exchange("grp", members, lambda j: q_out.at[j], lambda j: q_in.at[j], lambda j: q_send.at[j], lambda j: q_recv.at[j])
 
+    def exchange_of(a, outs, ins, send, recv):
+        return Exchange("grp", members, lambda j: outs[a].at[j], lambda j: ins[a].at[j], lambda j: send.at[a, j], lambda j: recv.at[a, j])
+
     def key_exchange(a):
-        return Exchange(
-            "grp", members, lambda j: pages_out.at[j * owned + a], lambda j: keys.at[a, j], lambda j: keys_send.at[a, j], lambda j: keys_recv.at[a, j]
-        )
+        return exchange_of(a, (pages_out0, pages_out1), (keys0, keys1), keys_send, keys_recv)
 
     def part_exchange(a):
-        return Exchange(
-            "grp", members, lambda j: part_out.at[a, j], lambda j: part_in.at[a, j], lambda j: part_send.at[a, j], lambda j: part_recv.at[a, j]
-        )
+        return exchange_of(a, (part_out0, part_out1), (part_in0, part_in1), part_send, part_recv)
 
     one.start()
     one.own().start()
@@ -178,7 +185,10 @@
     def _():
         queries.start()
 
-    pages.start(0, EARLY)
+    @pl.when(me % 2 == 0)
+    def _():
+        pages.start(0, EARLY)
+
     pages.own().start()
     queries.own().start()
     one.finish()
@@ -189,12 +199,12 @@
     loop(groups, choose)
     two.start()
     two.own().start()
-    pages.start(EARLY, groups - 1)
 
     @pl.when(me % 2 == 0)
     def _():
+        pages.start(EARLY, groups - 1)
+
         queries.start()
-
 
     def find_slot(i):
         source = request_source[i]
@@ -205,25 +215,16 @@
         slots[i] = jnp.minimum(lax.fori_loop(0, requests, count, jnp.int32(0)), capacity - 1)
 
     loop(requests, find_slot)
-    pages.finish()
-
-    def pick(i):
-        pages_out[i] = pages_in[request_source[i], slots[i]]
-
-    loop(requests, pick)
-    for a in range(owned):
-        key_exchange(a).start()
-        key_exchange(a).own().start()
     two.finish()
 
     def place(j):
         pref[mine, rows_of(j), columns_of(j)] = two_in[j, pl.ds(0, 16)]
 
-    def place_rope(b):
-        pref[mine, pl.ds(pl.multiple_of(b * 16, 16), 16), pl.ds(latent, lanes)] = two_in[4 * b, pl.ds(16, 16)]
+    def place_rope(j):
+        pref[mine, pl.ds(shard, 16), columns_of(j)] = two_in[j, pl.ds(16, 16)]
 
     loop(groups, place)
-    loop(groups // 4, place_rope)
+    loop(4, place_rope)
 
     across = {"grp": z * 2 + 1 - y}
     up, down = {"grp": ((z + 1) % half) * 2 + y}, {"grp": ((z + half - 1) % half) * 2 + y}
@@ -247,14 +248,12 @@
     send_on(mine, 0, up)
     send_on(mine, 1, down)
     send_on(mine, 2, across)
-    width = pref.shape[2]
-
-    def attend(a):
+    def attend(a, earlier):
         rows = members * block
-        at = pl.ds(pl.multiple_of(a * block, block), block)
-        q = q_in[:, at, :].reshape(rows, width)[:, : latent + rope]
-        k = keys[a].reshape(members * depth, latent + rope)
-        s = contract_last(q, k) * score_scale
+        q = q_in[:, pl.ds(a * block, block), :].reshape(rows, latent + lanes)[:, : latent + rope]
+        k_lat = (keys0[:, :, pl.ds(0, latent)], keys1[...])[a].reshape(members * depth, latent)
+        k_rope = keys0[:, :, pl.ds(latent, lanes)].reshape(members * depth, lanes)[:, rope * a : rope * (a + 1)]
+        s = (contract_last(q[:, :latent], k_lat) + contract_last(q[:, latent:], k_rope)) * score_scale
         usable = lax.broadcasted_iota(jnp.int32, s.shape, 1) < private_len[mine * owned + a]
         s = jnp.where(usable, s, very_negative)
         fresh = new_latent[mine * owned + a].astype(jnp.float32)
@@ -267,7 +266,7 @@
         m = jnp.maximum(jnp.max(s, axis=1, keepdims=True), jnp.maximum(new_s[0], new_s[1]))
         e = jnp.where(usable, jnp.exp(s - m), 0.0)
         length = jnp.sum(e, axis=1, keepdims=True)
-        summed = jnp.dot(e.astype(jnp.bfloat16), k[:, :latent], preferred_element_type=jnp.float32)
+        summed = jnp.dot(e.astype(jnp.bfloat16), k_lat, preferred_element_type=jnp.float32)
         for u in range(2):
             e_u = jnp.where(step >= u, jnp.exp(new_s[u] - m), 0.0)
             length = length + e_u
@@ -277,15 +276,19 @@
         middle = (lse - high).astype(jnp.bfloat16).astype(jnp.float32)
         low = lse - high - middle
         place = lax.broadcasted_iota(jnp.int32, (rows, lanes), 1)
-        tail = jnp.where(place == 0, high, jnp.where(place == 1, middle, jnp.where(place == 2, low, 0.0)))
-        part_out[a, :, :, pl.ds(0, latent)] = (summed / length).astype(jnp.bfloat16).reshape(members, block, latent)
-        part_out[a, :, :, pl.ds(latent, lanes)] = tail.astype(jnp.bfloat16).reshape(members, block, lanes)
-
-    def attend_and_send(a):
-        key_exchange(a).finish()
-        attend(a)
-        part_exchange(a).start()
-        part_exchange(a).own().start()
+        tail = jnp.where(place == 3 * a, high, jnp.where(place == 3 * a + 1, middle, jnp.where(place == 3 * a + 2, low, earlier)))
+        (part_out0, part_out1)[a][:, :, pl.ds(0, latent)] = (summed / length).astype(jnp.bfloat16).reshape(members, block, latent)
+        if a == 1:
+            part_out1[:, :, pl.ds(latent, lanes)] = tail.astype(jnp.bfloat16).reshape(members, block, lanes)
+        return tail
+
+    def attend_both():
+        tail = 0.0
+        for a in range(2):
+            key_exchange(a).finish()
+            tail = attend(a, tail)
+            part_exchange(a).start()
+            part_exchange(a).own().start()
 
     tile = scores.shape[2]
     rows = q_lat.shape[0]
@@ -293,21 +296,17 @@
     total[...] = jnp.zeros_like(total)
     weighted[...] = jnp.zeros_like(weighted)
 
-    def score(i):
-        k = pref[pl.ds(2 * i, 2)].reshape(tile, width)
-        s = contract_last(q_out[...].reshape(rows, width), k) * score_scale
-        scores[i] = s
-        top[...] = jnp.maximum(top[...], jnp.max(s, axis=1, keepdims=True))
-
-    def attend_at(hop):
-        if hop == ATTEND_AFTER:
-            queries.finish()
-            loop(owned, attend_and_send)
+    def odd_pages(hop):
+        if hop == ODD_PAGES:
+
+            @pl.when(me % 2 == 1)
+            def _():
+                pages.start()
 
     arrived(other)
     send_on(other, 0, up)
     send_on(other, 1, down)
-    attend_at(0)
+    odd_pages(0)
     for hop in (1, 2, 3):
         for column in (0, 1):
             c = shard_of(-hop, column)
@@ -318,39 +317,64 @@
             arrived(c)
             if hop < 3 or column == 1:
                 send_on(c, 1, down)
-        attend_at(hop)
+        odd_pages(hop)
     for column in (0, 1):
         arrived(shard_of(4, column))
+
+    def score(i):
+        k_lat = pref[pl.ds(2 * i, 2), pl.ds(0, shard)].reshape(tile, latent)
+        packed = [pref[2 * i + n, pl.ds(shard, 16)] for n in range(2)]
+        k_rope = jnp.concatenate([p[:, rope * b : rope * (b + 1)] for p in packed for b in range(shard // 16)], axis=0)
+        q = q_out[...].reshape(rows, latent + lanes)
+        s = (contract_last(q[:, :latent], k_lat) + contract_last(q[:, latent : latent + rope], k_rope)) * score_scale
+        scores[i] = s
+        top[...] = jnp.maximum(top[...], jnp.max(s, axis=1, keepdims=True))
+
+    pages.finish()
+
+    def pick(j):
+        first, second = [pages_in[request_source[2 * j + a], slots[2 * j + a]] for a in range(2)]
+        pages_out0[j, :, pl.ds(0, latent)] = first[:, :latent]
+        pages_out0[j, :, pl.ds(latent, lanes)] = jnp.concatenate([first[:, latent:], second[:, latent:]], axis=1)
+        pages_out1[j] = second[:, :latent]
+
+    loop(members, pick)
+    for a in range(2):
+        key_exchange(a).start()
+        key_exchange(a).own().start()
+
     loop(half, score)
 
     def weigh(i):
         e = jnp.exp(scores[i] - top[...])
         total[...] += jnp.sum(e, axis=1, keepdims=True)
-        k = pref[pl.ds(2 * i, 2), :, pl.ds(0, latent)].reshape(tile, latent)
+        k = pref[pl.ds(2 * i, 2), pl.ds(0, shard)].reshape(tile, latent)
         weighted[...] += jnp.dot(e.astype(jnp.bfloat16), k, preferred_element_type=jnp.float32)
 
     loop(half, weigh)
+    queries.finish()
+    attend_both()
 
     def merge(a, j):
         at = pl.ds(pl.multiple_of(j * own_rows + a * block, block), block)
-        tail = part_in[a, j, :, pl.ds(latent, lanes)].astype(jnp.float32)
-        lse = jnp.sum(tail, axis=1, keepdims=True)
-        part = part_in[a, j, :, pl.ds(0, latent)].astype(jnp.float32)
+        tail = part_in1[j, :, pl.ds(latent, lanes)].astype(jnp.float32)
+        mine_of_tail = lax.broadcasted_iota(jnp.int32, tail.shape, 1) // 3 == a
+        lse = jnp.sum(jnp.where(mine_of_tail, tail, 0.0), axis=1, keepdims=True)
+        part = (part_in0[j], part_in1[j, :, pl.ds(0, latent)])[a].astype(jnp.float32)
         m = jnp.maximum(top[at], lse)
         scale, part_scale = jnp.exp(top[at] - m), jnp.exp(lse - m)
         share = 1.0 / (total[at] * scale + part_scale)
         out[at] = (weighted[at] * (scale * share) + part * (part_scale * share)).astype(jnp.bfloat16)
 
-    def merge_all(a):
-        part_exchange(a).finish()
-
-        def four(i):
-            for j in range(4):
-                merge(a, 4 * i + j)
-
-        loop(members // 4, four)
-
-    loop(owned, merge_all)
+    part_exchange(0).finish()
+    part_exchange(1).finish()
+
+    def merge_two(i):
+        for j in range(2):
+            for a in range(2):
+                merge(a, 2 * i + j)
+
+    loop(members // 2, merge_two)
     for exchange in [one, two, pages, queries] + [f(a) for a in range(owned) for f in (key_exchange, part_exchange)]:
         exchange.drain()
     for c, way, where in sends:
@@ -373,21 +397,21 @@
     return pl.pallas_call(
         functools.partial(kernel, groups, members),
         out_shape=jax.ShapeDtypeStruct((rows, latent), bf16),
-        in_specs=[vmem, vmem, vmem, vmem, vmem, smem, smem, anywhere, smem, smem],
+        in_specs=[vmem, vmem, vmem, vmem, smem, smem, anywhere, smem, smem],
         out_specs=vmem,
         scratch_shapes=[pltpu.VMEM((members, own, wide), bf16)] * 2
         + [pltpu.VMEM((groups, 32, lanes), bf16)] * 4
         + [
-            pltpu.VMEM((members, shard, wide), bf16),
+            pltpu.VMEM((members, shard + 16, latent), bf16),
             pltpu.VMEM((members // 2, rows, 2 * shard), f32),
             pltpu.VMEM((rows, latent), f32),
             pltpu.VMEM((rows, 1), f32),
             pltpu.VMEM((rows, 1), f32),
             pltpu.VMEM((groups, capacity, depth, width), bf16),
-            pltpu.VMEM((requests, depth, width), bf16),
-            pltpu.VMEM((owned, members, depth, width), bf16),
-            pltpu.VMEM((owned, members, own // owned, wide), bf16),
-            pltpu.VMEM((owned, members, own // owned, wide), bf16),
+        ]
+        + [pltpu.VMEM((members, depth, w), bf16) for w in (wide, latent)] * 2
+        + [pltpu.VMEM((members, own // owned, w), bf16) for w in (latent, wide)] * 2
+        + [
             pltpu.SMEM((requests,), jnp.int32),
         ]
         + [dma((groups,))] * 4
@@ -396,14 +420,13 @@
         + [dma((owned, members))] * 2
         + [dma((members,))] * 2
         + [dma((owned, members))] * 2,
-        compiler_params=pltpu.CompilerParams(collective_id=0, has_side_effects=True, vmem_limit_bytes=40 * MIB),
+        compiler_params=pltpu.CompilerParams(collective_id=0, has_side_effects=True, vmem_limit_bytes=24 * MIB),
         cost_estimate=pl.CostEstimate(flops=2_700_000_000, bytes_accessed=8_000_000, transcendentals=2_000_000),
     )(
         q_lat,
         q_rope,
         new_latent,
-        prefix_shard[:, :latent],
-        prefix_shard[:, latent:],
+        prefix_shard,
         store_order,
         prefix_of_group,
         private_store,

time: 137 us -> 123 us (0.90)
  the two profiles are of different devices: /device:TPU:30 before, /device:TPU:22 now
where the time goes in v4:
time: 123 us
  Pallas kernels  119 us (97%)
  local copies, waits for them, and re-layouts  2.38 us (2%)
  matrix products  2.02 us (2%)
    pallas_call x1, Pallas kernels, attention(): pl.pallas_call(functools.partial(kernel, groups, members), out_shape=jax....  119 us

profile of v4, /device:TPU:22, one launch (start us, length us, event | category | flops | bytes accessed | tf_op | source)
XLA Modules:
  0.0 123.2 jit_solution(6161306534358261405)
XLA Ops:
  0.0 0.0 copy-start
  0.0 1.1 copy.14
  1.2 0.1 copy-done
  1.3 0.0 copy-start.1
  1.3 0.0 copy-start.2
  1.3 0.0 copy-start.3
  1.3 0.0 copy-start.4
  1.3 0.0 copy-start.5
  1.3 0.0 copy-start.6
  1.3 0.0 copy-start.7
  1.3 1.3 %fusion = bf16[32,2,8,512]{3,0,1,2:T(8,128)(2,1)S(1)} fusion(bf16[8,128,512]{2,1,0:T(8,128)(2,1)S(1)} %copy-done, bf16[32,2,8,128]{3,2,1,0:T(8,128)(2,1)} %param.11), kind=kOutput, calls=%fused_computation.1 | convolution fusion | flops 67371008 | bytes 1703936 | tf_op jit(solution)/shard_map/rthn,hnc->rthc/dot_general | solution.py:454
  2.7 0.3 copy.13
  3.0 0.0 copy-done.1
  3.0 0.0 copy-done.2
  3.0 0.0 copy-done.3
  3.0 0.0 copy-done.4
  3.0 0.0 copy-done.5
  3.0 0.0 copy-done.6
  3.0 0.0 copy-done.7
  3.0 0.0 copy-start.8
  3.0 118.6 %shard_map.109 = bf16[512,512]{1,0:T(8,128)(2,1)S(1)} custom-call(bf16[512,512]{1,0:T(8,128)(2,1)S(1)} %bitcast.21, bf16[512,64]{1,0:T(8,128)(2,1)S(1)} %bitcast.25, bf16[32,2,576]{2,1,0:T(2,128)(2,1)S(1)} %copy-done.3, bf16[128,576]{1,0:T(8,128)(2,1)S(1)} %bitcast.23, s32[32]{0:T(128)S(1)} %copy-done.4, s32[32]{0:T(128)S(1)} %copy-done.5, ...), custom_call_target="tpu_custom_call" | custom-call | flops 2700000000 | bytes 8000000 | tf_op jit(solution)/shard_map/pallas_call | solution.py:397
  121.7 0.0 copy-done.8
  121.7 0.7 fusion.1
  122.4 0.8 copy.16
Async XLA Ops:
  0.0 1.3 %copy-start = (bf16[8,128,512]{2,1,0:T(8,128)(2,1)S(1)}, bf16[8,128,512]{2,1,0:T(8,128)(2,1)}, u32[]{:S(2)}) copy-start(bf16[8,128,512]{2,1,0:T(8,128)(2,1)} %param.14) | copy-start | bytes 3145732
  1.3 1.7 %copy-start.1 = (bf16[1,32,2,16,576]{4,3,2,1,0:T(8,128)(2,1)S(1)}, bf16[1,32,2,16,576]{4,3,2,1,0:T(8,128)(2,1)}, u32[]{:S(2)}) copy-start(bf16[1,32,2,16,576]{4,3,2,1,0:T(8,128)(2,1)} %param.19) | copy-start | bytes 3538948
  1.3 1.7 %copy-start.2 = (bf16[32,2,8,64]{3,2,1,0:T(8,128)(2,1)S(1)}, bf16[32,2,8,64]{3,2,1,0:T(8,128)(2,1)}, u32[]{:S(2)}) copy-start(bf16[32,2,8,64]{3,2,1,0:T(8,128)(2,1)} %param.12) | copy-start | bytes 196612
  1.3 1.7 %copy-start.3 = (bf16[32,2,576]{2,1,0:T(2,128)(2,1)S(1)}, bf16[32,2,576]{2,1,0:T(2,128)(2,1)}, u32[]{:S(2)}) copy-start(bf16[32,2,576]{2,1,0:T(2,128)(2,1)} %new_latent.1) | copy-start | bytes 221188
  1.3 1.7 %copy-start.4 = (s32[32]{0:T(128)S(1)}, s32[32]{0:T(128)}, u32[]{:S(2)}) copy-start(s32[32]{0:T(128)} %store_order.1) | copy-start | bytes 388
  1.3 1.7 %copy-start.5 = (s32[32]{0:T(128)S(1)}, s32[32]{0:T(128)}, u32[]{:S(2)}) copy-start(s32[32]{0:T(128)} %prefix_of_group.1) | copy-start | bytes 388
  1.3 1.7 %copy-start.6 = (s32[32,1]{0,1:T(1,128)S(1)}, s32[32,1]{0,1:T(1,128)}, u32[]{:S(2)}) copy-start(s32[32,1]{0,1:T(1,128)} %param.20) | copy-start | bytes 388
  1.3 1.7 %copy-start.7 = (s32[1,32]{1,0:T(1,128)S(1)}, s32[1,32]{1,0:T(1,128)}, u32[]{:S(2)}) copy-start(s32[1,32]{1,0:T(1,128)} %param.21) | copy-start | bytes 388
  3.0 118.7 %copy-start.8 = (bf16[8,512,128]{2,1,0:T(8,128)(2,1)S(1)}, bf16[8,512,128]{2,1,0:T(8,128)(2,1)}, u32[]{:S(2)}) copy-start(bf16[8,512,128]{2,1,0:T(8,128)(2,1)} %param.15) | copy-start | bytes 3145732

commit v5 on v4

--- a/solution.py
+++ b/solution.py
@@ -11,8 +11,9 @@
 very_negative = -1e30
 MIB = 1024 * 1024
 MESH = pl.DeviceIdType.MESH
-EARLY = 12
+EARLY = 16
 ODD_PAGES = 1
+PICK_AFTER = 3
 
 
 def contract_last(a, b):
@@ -54,7 +55,8 @@
         self.me = lax.axis_index(axis)
 
     def peer(self, k):
-        return (self.me + k + 1) % self.peers
+        away = (k // 2 + 1) * (1 - 2 * (k % 2)) if self.axis == "grp" else k + 1
+        return (self.me + self.peers + away) % self.peers
 
     def to(self, j):
         return remote(self.out_ref(j), self.in_ref(self.me), self.send(j), self.recv(self.me), {self.axis: j})
@@ -303,6 +305,20 @@
             def _():
                 pages.start()
 
+    def send_keys():
+        pages.finish()
+
+        def pick(j):
+            first, second = [pages_in[request_source[2 * j + a], slots[2 * j + a]] for a in range(2)]
+            pages_out0[j, :, pl.ds(0, latent)] = first[:, :latent]
+            pages_out0[j, :, pl.ds(latent, lanes)] = jnp.concatenate([first[:, latent:], second[:, latent:]], axis=1)
+            pages_out1[j] = second[:, :latent]
+
+        loop(members, pick)
+        for a in range(2):
+            key_exchange(a).start()
+            key_exchange(a).own().start()
+
     arrived(other)
     send_on(other, 0, up)
     send_on(other, 1, down)
@@ -318,6 +334,8 @@
             if hop < 3 or column == 1:
                 send_on(c, 1, down)
         odd_pages(hop)
+        if hop == PICK_AFTER:
+            send_keys()
     for column in (0, 1):
         arrived(shard_of(4, column))
 
@@ -329,19 +347,6 @@
         s = (contract_last(q[:, :latent], k_lat) + contract_last(q[:, latent : latent + rope], k_rope)) * score_scale
         scores[i] = s
         top[...] = jnp.maximum(top[...], jnp.max(s, axis=1, keepdims=True))
-
-    pages.finish()
-
-    def pick(j):
-        first, second = [pages_in[request_source[2 * j + a], slots[2 * j + a]] for a in range(2)]
-        pages_out0[j, :, pl.ds(0, latent)] = first[:, :latent]
-        pages_out0[j, :, pl.ds(latent, lanes)] = jnp.concatenate([first[:, latent:], second[:, latent:]], axis=1)
-        pages_out1[j] = second[:, :latent]
-
-    loop(members, pick)
-    for a in range(2):
-        key_exchange(a).start()
-        key_exchange(a).own().start()
 
     loop(half, score)
 

time: 123 us -> 121 us (0.984)
  the two profiles are of different devices: /device:TPU:22 before, /device:TPU:6 now
where the time goes in v5:
time: 121 us; the launch traced here: 119 us
  Pallas kernels  115 us (95%)
  local copies, waits for them, and re-layouts  2.38 us (2%)
  matrix products  2.02 us (2%)
    pallas_call x1, Pallas kernels, attention(): pl.pallas_call(functools.partial(kernel, groups, members), out_shape=jax....  115 us

profile of v5, /device:TPU:6, one launch (start us, length us, event | category | flops | bytes accessed | tf_op | source)
XLA Modules:
  0.0 119.4 jit_solution(791528637364215706)
XLA Ops:
  0.0 0.0 copy-start
  0.0 1.1 copy.14
  1.2 0.1 copy-done
  1.3 0.0 copy-start.1
  1.3 0.0 copy-start.2
  1.3 0.0 copy-start.3
  1.3 0.0 copy-start.4
  1.3 0.0 copy-start.5
  1.3 0.0 copy-start.6
  1.3 0.0 copy-start.7
  1.3 1.3 %fusion = bf16[32,2,8,512]{3,0,1,2:T(8,128)(2,1)S(1)} fusion(bf16[8,128,512]{2,1,0:T(8,128)(2,1)S(1)} %copy-done, bf16[32,2,8,128]{3,2,1,0:T(8,128)(2,1)} %param.11), kind=kOutput, calls=%fused_computation.1 | convolution fusion | flops 67371008 | bytes 1703936 | tf_op jit(solution)/shard_map/rthn,hnc->rthc/dot_general | solution.py:459
  2.7 0.3 copy.13
  3.0 0.0 copy-done.1
  3.0 0.0 copy-done.2
  3.0 0.0 copy-done.3
  3.0 0.0 copy-done.4
  3.0 0.0 copy-done.5
  3.0 0.0 copy-done.6
  3.0 0.0 copy-done.7
  3.0 0.0 copy-start.8
  3.0 114.9 %shard_map.109 = bf16[512,512]{1,0:T(8,128)(2,1)S(1)} custom-call(bf16[512,512]{1,0:T(8,128)(2,1)S(1)} %bitcast.21, bf16[512,64]{1,0:T(8,128)(2,1)S(1)} %bitcast.25, bf16[32,2,576]{2,1,0:T(2,128)(2,1)S(1)} %copy-done.3, bf16[128,576]{1,0:T(8,128)(2,1)S(1)} %bitcast.23, s32[32]{0:T(128)S(1)} %copy-done.4, s32[32]{0:T(128)S(1)} %copy-done.5, ...), custom_call_target="tpu_custom_call" | custom-call | flops 2700000000 | bytes 8000000 | tf_op jit(solution)/shard_map/pallas_call | solution.py:402
  118.0 0.0 copy-done.8
  118.0 0.7 fusion.1
  118.7 0.8 copy.16
Async XLA Ops:
  0.0 1.3 %copy-start = (bf16[8,128,512]{2,1,0:T(8,128)(2,1)S(1)}, bf16[8,128,512]{2,1,0:T(8,128)(2,1)}, u32[]{:S(2)}) copy-start(bf16[8,128,512]{2,1,0:T(8,128)(2,1)} %param.14) | copy-start | bytes 3145732
  1.3 1.7 %copy-start.1 = (bf16[1,32,2,16,576]{4,3,2,1,0:T(8,128)(2,1)S(1)}, bf16[1,32,2,16,576]{4,3,2,1,0:T(8,128)(2,1)}, u32[]{:S(2)}) copy-start(bf16[1,32,2,16,576]{4,3,2,1,0:T(8,128)(2,1)} %param.19) | copy-start | bytes 3538948
  1.3 1.7 %copy-start.2 = (bf16[32,2,8,64]{3,2,1,0:T(8,128)(2,1)S(1)}, bf16[32,2,8,64]{3,2,1,0:T(8,128)(2,1)}, u32[]{:S(2)}) copy-start(bf16[32,2,8,64]{3,2,1,0:T(8,128)(2,1)} %param.12) | copy-start | bytes 196612
  1.3 1.7 %copy-start.3 = (bf16[32,2,576]{2,1,0:T(2,128)(2,1)S(1)}, bf16[32,2,576]{2,1,0:T(2,128)(2,1)}, u32[]{:S(2)}) copy-start(bf16[32,2,576]{2,1,0:T(2,128)(2,1)} %new_latent.1) | copy-start | bytes 221188
  1.3 1.7 %copy-start.4 = (s32[32]{0:T(128)S(1)}, s32[32]{0:T(128)}, u32[]{:S(2)}) copy-start(s32[32]{0:T(128)} %store_order.1) | copy-start | bytes 388
  1.3 1.7 %copy-start.5 = (s32[32]{0:T(128)S(1)}, s32[32]{0:T(128)}, u32[]{:S(2)}) copy-start(s32[32]{0:T(128)} %prefix_of_group.1) | copy-start | bytes 388
  1.3 1.7 %copy-start.6 = (s32[32,1]{0,1:T(1,128)S(1)}, s32[32,1]{0,1:T(1,128)}, u32[]{:S(2)}) copy-start(s32[32,1]{0,1:T(1,128)} %param.20) | copy-start | bytes 388
  1.3 1.7 %copy-start.7 = (s32[1,32]{1,0:T(1,128)S(1)}, s32[1,32]{1,0:T(1,128)}, u32[]{:S(2)}) copy-start(s32[1,32]{1,0:T(1,128)} %param.21) | copy-start | bytes 388
  3.0 114.9 %copy-start.8 = (bf16[8,512,128]{2,1,0:T(8,128)(2,1)S(1)}, bf16[8,512,128]{2,1,0:T(8,128)(2,1)}, u32[]{:S(2)}) copy-start(bf16[8,512,128]{2,1,0:T(8,128)(2,1)} %param.15) | copy-start | bytes 3145732

commit v6 on v5

--- a/solution.py
+++ b/solution.py
@@ -371,6 +371,10 @@
         share = 1.0 / (total[at] * scale + part_scale)
         out[at] = (weighted[at] * (scale * share) + part * (part_scale * share)).astype(jnp.bfloat16)
 
+    for exchange in (one, two, pages, queries, key_exchange(0), key_exchange(1)):
+        exchange.drain()
+    for c, way, where in sends:
+        ring(c, way, where).wait_send()
     part_exchange(0).finish()
     part_exchange(1).finish()
 
@@ -380,10 +384,8 @@
                 merge(a, 2 * i + j)
 
     loop(members // 2, merge_two)
-    for exchange in [one, two, pages, queries] + [f(a) for a in range(owned) for f in (key_exchange, part_exchange)]:
-        exchange.drain()
-    for c, way, where in sends:
-        ring(c, way, where).wait_send()
+    for a in range(2):
+        part_exchange(a).drain()
 
 
 def attention(members, q_lat, q_rope, new_latent, prefix_shard, store_order, prefix_of_group, private_store, request_source, private_len):

time: 121 us -> 119 us (0.983)
  Pallas kernels: 115 us -> 113 us
    pallas_call x1, Pallas kernels: 115 us -> 113 us  [attention(): pl.pallas_call(functools.partial(kernel, groups, members), out_shape=jax....]
where the time goes in v6:
time: 119 us; the launch traced here: 117 us
  Pallas kernels  113 us (95%)
  local copies, waits for them, and re-layouts  2.38 us (2%)
  matrix products  2.02 us (2%)
    pallas_call x1, Pallas kernels, attention(): pl.pallas_call(functools.partial(kernel, groups, members), out_shape=jax....  113 us

profile of v6, /device:TPU:6, one launch (start us, length us, event | category | flops | bytes accessed | tf_op | source)
XLA Modules:
  0.0 117.5 jit_solution(2765132509809200789)
XLA Ops:
  0.0 0.0 copy-start
  0.0 1.1 copy.14
  1.2 0.1 copy-done
  1.3 0.0 copy-start.1
  1.3 0.0 copy-start.2
  1.3 0.0 copy-start.3
  1.3 0.0 copy-start.4
  1.3 0.0 copy-start.5
  1.3 0.0 copy-start.6
  1.3 0.0 copy-start.7
  1.3 1.3 %fusion = bf16[32,2,8,512]{3,0,1,2:T(8,128)(2,1)S(1)} fusion(bf16[8,128,512]{2,1,0:T(8,128)(2,1)S(1)} %copy-done, bf16[32,2,8,128]{3,2,1,0:T(8,128)(2,1)} %param.11), kind=kOutput, calls=%fused_computation.1 | convolution fusion | flops 67371008 | bytes 1703936 | tf_op jit(solution)/shard_map/rthn,hnc->rthc/dot_general | solution.py:461
  2.7 0.3 copy.13
  3.0 0.0 copy-done.1
  3.0 0.0 copy-done.2
  3.0 0.0 copy-done.3
  3.0 0.0 copy-done.4
  3.0 0.0 copy-done.5
  3.0 0.0 copy-done.6
  3.0 0.0 copy-done.7
  3.0 0.0 copy-start.8
  3.0 112.9 %shard_map.109 = bf16[512,512]{1,0:T(8,128)(2,1)S(1)} custom-call(bf16[512,512]{1,0:T(8,128)(2,1)S(1)} %bitcast.21, bf16[512,64]{1,0:T(8,128)(2,1)S(1)} %bitcast.25, bf16[32,2,576]{2,1,0:T(2,128)(2,1)S(1)} %copy-done.3, bf16[128,576]{1,0:T(8,128)(2,1)S(1)} %bitcast.23, s32[32]{0:T(128)S(1)} %copy-done.4, s32[32]{0:T(128)S(1)} %copy-done.5, ...), custom_call_target="tpu_custom_call" | custom-call | flops 2700000000 | bytes 8000000 | tf_op jit(solution)/shard_map/pallas_call | solution.py:404
  116.0 0.0 copy-done.8
  116.0 0.7 fusion.1
  116.7 0.8 copy.16
Async XLA Ops:
  0.0 1.3 %copy-start = (bf16[8,128,512]{2,1,0:T(8,128)(2,1)S(1)}, bf16[8,128,512]{2,1,0:T(8,128)(2,1)}, u32[]{:S(2)}) copy-start(bf16[8,128,512]{2,1,0:T(8,128)(2,1)} %param.14) | copy-start | bytes 3145732
  1.3 1.7 %copy-start.1 = (bf16[1,32,2,16,576]{4,3,2,1,0:T(8,128)(2,1)S(1)}, bf16[1,32,2,16,576]{4,3,2,1,0:T(8,128)(2,1)}, u32[]{:S(2)}) copy-start(bf16[1,32,2,16,576]{4,3,2,1,0:T(8,128)(2,1)} %param.19) | copy-start | bytes 3538948
  1.3 1.7 %copy-start.2 = (bf16[32,2,8,64]{3,2,1,0:T(8,128)(2,1)S(1)}, bf16[32,2,8,64]{3,2,1,0:T(8,128)(2,1)}, u32[]{:S(2)}) copy-start(bf16[32,2,8,64]{3,2,1,0:T(8,128)(2,1)} %param.12) | copy-start | bytes 196612
  1.3 1.7 %copy-start.3 = (bf16[32,2,576]{2,1,0:T(2,128)(2,1)S(1)}, bf16[32,2,576]{2,1,0:T(2,128)(2,1)}, u32[]{:S(2)}) copy-start(bf16[32,2,576]{2,1,0:T(2,128)(2,1)} %new_latent.1) | copy-start | bytes 221188
  1.3 1.7 %copy-start.4 = (s32[32]{0:T(128)S(1)}, s32[32]{0:T(128)}, u32[]{:S(2)}) copy-start(s32[32]{0:T(128)} %store_order.1) | copy-start | bytes 388
  1.3 1.7 %copy-start.5 = (s32[32]{0:T(128)S(1)}, s32[32]{0:T(128)}, u32[]{:S(2)}) copy-start(s32[32]{0:T(128)} %prefix_of_group.1) | copy-start | bytes 388
  1.3 1.7 %copy-start.6 = (s32[32,1]{0,1:T(1,128)S(1)}, s32[32,1]{0,1:T(1,128)}, u32[]{:S(2)}) copy-start(s32[32,1]{0,1:T(1,128)} %param.20) | copy-start | bytes 388
  1.3 1.7 %copy-start.7 = (s32[1,32]{1,0:T(1,128)S(1)}, s32[1,32]{1,0:T(1,128)}, u32[]{:S(2)}) copy-start(s32[1,32]{1,0:T(1,128)} %param.21) | copy-start | bytes 388
  3.0 113.0 %copy-start.8 = (bf16[8,512,128]{2,1,0:T(8,128)(2,1)S(1)}, bf16[8,512,128]{2,1,0:T(8,128)(2,1)}, u32[]{:S(2)}) copy-start(bf16[8,512,128]{2,1,0:T(8,128)(2,1)} %param.15) | copy-start | bytes 3145732
